TPU v7x, 128 devices: a whole 4x4x4 slice. The times are simulated.
128 devices in a mesh: seq: 32 (over x_lo, z, y), head: 4 (over x_hi, core).
Axes of the slice: x: 4 (x_hi: 2, x_lo: 2; x = x_hi * 2 + x_lo), y: 4, z: 4, core: 2. Of those that a mesh axis runs over, the one named last changes fastest.
Arguments:
- queries: bfloat16 [4096, 3584], P('seq', 'head'), may hold values from -80 to 80
- key_vectors: bfloat16 [4096, 512], P('seq', 'head'), may hold values from -4 to 4
- value_vectors: bfloat16 [4096, 512], P('seq', 'head'), may hold values from -10 to 10
- out_cotangent: bfloat16 [4096, 3584], P('seq', 'head'), may hold values from -6 to 6
- latent_mask: int32 [4096], P('seq'), may hold values from 0 to 1, as said below
- clean_latents: float32 [2048, 64], P('seq'), may hold values from -6 to 6
- noise_draws: float32 [2048, 256], P('seq'), may hold values from -6 to 6
- timesteps: int32 [2048, 4], P('seq'), may hold values from 0 to 999
- latent_in: bfloat16 [64, 3584], replicated, may hold values from -0.75 to 0.75
- norm_gain: float32 [3584], replicated, may hold values from 0.1 to 1.9
- gate_weight: bfloat16 [3584, 5632], P('seq', 'head'), may hold values from -0.09375 to 0.09375
- up_weight: bfloat16 [3584, 5632], P('seq', 'head'), may hold values from -0.09375 to 0.09375
- down_weight: bfloat16 [3584, 5632], P('seq', 'head'), may hold values from -0.078125 to 0.078125
- out_gain: float32 [3584], replicated, may hold values from 0.1 to 1.9
- latent_out: bfloat16 [3584, 64], replicated, may hold values from -0.09375 to 0.09375
Outputs:
- attention_out: bfloat16 [4096, 3584], P('seq', 'head')
- grad_queries: bfloat16 [4096, 3584], P('seq', 'head')
- grad_keys: bfloat16 [4096, 512], P('seq', 'head')
- grad_values: bfloat16 [4096, 512], P('seq', 'head')
- prediction: float32 [2048, 256], P('seq', 'head')
Inputs may be any that keep to these rules, and one draw needn't show every extreme that they name: `latent_mask`: within each block of 128 positions the positions with mask 1 form one contiguous run of 64/4 (rounded down) to 64 positions; in every draw some block holds exactly 64.
All inputs are finite; a program needn't handle non-finite values.
Results may differ from a plain program's by a relative error of at most 0.035.
Values may be sent and summed in bfloat16 or wider, within the bound.
A program may use at most 128 MiB of HBM per device.

v0:
```python
import math

import jax
import jax.numpy as jnp
from jax import lax
from jax.sharding import PartitionSpec as P

HEADS = 28
KVH = 4
HD = 128
D = 3584
NOISE = 4


def block_width(row_count):
    return math.gcd(row_count, 512)


def score_block(query_rows, key_block, query_pos, key_pos):
    score_scale = 1.0 / math.sqrt(query_rows.shape[-1])
    scores = (
        jnp.einsum("qgjd,kgd->gjqk", query_rows, key_block, preferred_element_type=jnp.float32)
        * score_scale
    )
    allowed = (key_pos[None, :] <= query_pos[:, None])[None, None]
    return (scores, allowed)


def attend_piece(softmax_state, key_piece, value_piece, query_rows, query_pos):
    row_count = key_piece.shape[0]
    block_rows = block_width(row_count)
    groups = query_rows.shape[1]
    head_dim = query_rows.shape[3]

    def attend_advance(step_index, loop_state):
        offset = step_index * block_rows

        def attend_compute(current):
            run_max, run_total, weighted_sum = current
            key_block = lax.dynamic_slice_in_dim(key_piece, offset, block_rows, 0).reshape(
                block_rows, groups, head_dim
            )
            value_block = lax.dynamic_slice_in_dim(value_piece, offset, block_rows, 0).reshape(
                block_rows, groups, head_dim
            )
            key_pos = offset + jnp.arange(block_rows, dtype=jnp.int32)
            scores, allowed = score_block(query_rows, key_block, query_pos, key_pos)
            new_max = jnp.maximum(run_max, jnp.max(jnp.where(allowed, scores, -jnp.inf), axis=-1))
            soft_exp = jnp.where(allowed, jnp.exp(scores - new_max[..., None]), 0.0)
            factor = jnp.exp(run_max - new_max)
            new_total = run_total * factor + jnp.sum(soft_exp, axis=-1)
            update = jnp.einsum(
                "gjqk,kgd->gjqd",
                soft_exp.astype(jnp.bfloat16),
                value_block,
                preferred_element_type=jnp.float32,
            )
            return (new_max, new_total, weighted_sum * factor[..., None] + update)

        return lax.cond(
            offset <= query_pos[-1], attend_compute, lambda current: current, loop_state
        )

    return lax.fori_loop(0, row_count // block_rows, attend_advance, softmax_state)


def backward_sweep(key_buf, value_buf, row_count, query_side):
    query_rows, grad_rows, log_total, row_delta, query_pos = query_side
    block_rows = block_width(row_count)
    local_rows = query_rows.shape[0]
    groups = query_rows.shape[1]
    per_group = query_rows.shape[2]
    head_dim = query_rows.shape[3]
    pair_width = groups * head_dim
    score_scale = 1.0 / math.sqrt(head_dim)
    query_start = jnp.zeros((groups, per_group, local_rows, head_dim), jnp.float32)
    term_start = jnp.zeros((row_count, 2 * pair_width), jnp.float32)

    def backward_advance(step_index, loop_state):
        offset = step_index * block_rows

        def backward_compute(current):
            query_sum, term_sum = current
            key_block = lax.dynamic_slice_in_dim(key_buf, offset, block_rows, 0).reshape(
                block_rows, groups, head_dim
            )
            value_block = lax.dynamic_slice_in_dim(value_buf, offset, block_rows, 0).reshape(
                block_rows, groups, head_dim
            )
            key_pos = offset + jnp.arange(block_rows, dtype=jnp.int32)
            scores, allowed = score_block(query_rows, key_block, query_pos, key_pos)
            soft_weights = jnp.where(allowed, jnp.exp(scores - log_total[..., None]), 0.0)
            grad_weights = jnp.einsum(
                "qgjd,kgd->gjqk", grad_rows, value_block, preferred_element_type=jnp.float32
            )
            grad_scores = (soft_weights * (grad_weights - row_delta[..., None])).astype(
                jnp.bfloat16
            )
            query_sum = query_sum + jnp.einsum(
                "gjqk,kgd->gjqd", grad_scores, key_block, preferred_element_type=jnp.float32
            )
            key_term = (
                jnp.einsum(
                    "gjqk,qgjd->kgd", grad_scores, query_rows, preferred_element_type=jnp.float32
                )
                * score_scale
            )
            value_term = jnp.einsum(
                "gjqk,qgjd->kgd",
                soft_weights.astype(jnp.bfloat16),
                grad_rows,
                preferred_element_type=jnp.float32,
            )
            joined = jnp.concatenate(
                [
                    key_term.reshape(block_rows, pair_width),
                    value_term.reshape(block_rows, pair_width),
                ],
                axis=1,
            )
            term_sum = lax.dynamic_update_slice_in_dim(term_sum, joined, offset, 0)
            return (query_sum, term_sum)

        return lax.cond(
            offset <= query_pos[-1], backward_compute, lambda current: current, loop_state
        )

    return lax.fori_loop(0, row_count // block_rows, backward_advance, (query_start, term_start))


def rms_scale(rows, gain):
    return rows * lax.rsqrt(jnp.mean(rows * rows, axis=-1, keepdims=True) + 1e-06) * gain


def down_product(hidden, down_rows):
    return lax.dot_general(
        hidden, down_rows, (((1,), (1,)), ((), ())), preferred_element_type=jnp.float32
    )


def shards(
    queries,
    key_vectors,
    value_vectors,
    out_cotangent,
    latent_mask,
    clean_latents,
    noise_draws,
    timesteps,
    latent_in,
    norm_gain,
    gate_weight,
    up_weight,
    down_weight,
    out_gain,
    latent_out,
):
    local_rows = queries.shape[0]
    pair_width = key_vectors.shape[1]
    groups = pair_width // HD
    per_group = HEADS // KVH
    query_rows = queries.reshape(local_rows, groups, per_group, HD)
    grad_rows = out_cotangent.reshape(local_rows, groups, per_group, HD)
    query_pos = lax.axis_index("seq") * local_rows + jnp.arange(local_rows, dtype=jnp.int32)
    total_rows = local_rows * lax.axis_size("seq")
    start_state = (
        jnp.full((groups, per_group, local_rows), -1e30, jnp.float32),
        jnp.zeros((groups, per_group, local_rows), jnp.float32),
        jnp.zeros((groups, per_group, local_rows, HD), jnp.float32),
    )
    key_buf, value_buf = (
        lax.all_gather(key_vectors, "seq", axis=0, tiled=True),
        lax.all_gather(value_vectors, "seq", axis=0, tiled=True),
    )
    run_max, run_total, weighted_sum = attend_piece(
        start_state, key_buf, value_buf, query_rows, query_pos
    )
    attended = weighted_sum / run_total[..., None]
    attention_out = (
        jnp.transpose(attended, (2, 0, 1, 3))
        .reshape(local_rows, groups * per_group * HD)
        .astype(jnp.bfloat16)
    )
    log_total = run_max + jnp.log(run_total)
    out_rows = attention_out.reshape(local_rows, groups, per_group, HD)
    row_delta = jnp.einsum(
        "qgjd,qgjd->gjq", out_rows, grad_rows, preferred_element_type=jnp.float32
    )
    query_side = (query_rows, grad_rows, log_total, row_delta, query_pos)
    query_sum, all_terms = backward_sweep(key_buf, value_buf, total_rows, query_side)
    own_terms = lax.psum_scatter(
        all_terms.astype(jnp.bfloat16), "seq", scatter_dimension=0, tiled=True
    ).astype(jnp.float32)
    scaled = query_sum * (1.0 / math.sqrt(HD))
    grad_queries = (
        jnp.transpose(scaled, (2, 0, 1, 3))
        .reshape(local_rows, groups * per_group * HD)
        .astype(jnp.bfloat16)
    )
    grad_keys = own_terms[:, :pair_width].astype(jnp.bfloat16)
    grad_values = own_terms[:, pair_width:].astype(jnp.bfloat16)
    slot_count = clean_latents.shape[0]
    latent_dim = clean_latents.shape[1]
    slot_rank = jnp.cumsum(latent_mask, dtype=jnp.int32) - 1
    slot_ids = jnp.arange(slot_count, dtype=jnp.int32)
    chooser = ((slot_rank[None, :] == slot_ids[:, None]) & (latent_mask[None, :] == 1)).astype(
        jnp.bfloat16
    )
    local_condition = jnp.dot(chooser, attention_out, preferred_element_type=jnp.float32).astype(
        jnp.bfloat16
    )
    condition = lax.all_gather(local_condition, "head", axis=1, tiled=True)
    slot_valid = slot_ids < jnp.sum(latent_mask, dtype=jnp.int32)
    step_float = timesteps.astype(jnp.float32)
    signal_share = jnp.cos((step_float / 1000.0 + 0.008) / 1.008 * (math.pi / 2.0)) ** 2
    noise_rows = noise_draws.reshape(slot_count, NOISE, latent_dim)
    noisy_rows = (
        jnp.sqrt(signal_share)[..., None] * clean_latents[:, None, :]
        + jnp.sqrt(1.0 - signal_share)[..., None] * noise_rows
    )
    noisy_rows = (
        jnp.transpose(noisy_rows, (1, 0, 2))
        .reshape(NOISE * slot_count, latent_dim)
        .astype(jnp.bfloat16)
    )
    lifted = jnp.dot(noisy_rows, latent_in, preferred_element_type=jnp.float32)
    half_width = D // 2
    frequencies = jnp.exp(
        -math.log(10000.0) * jnp.arange(half_width, dtype=jnp.float32) / half_width
    )
    angles = jnp.transpose(step_float).reshape(NOISE * slot_count)[:, None] * frequencies[None, :]
    embedding = jnp.concatenate([jnp.cos(angles), jnp.sin(angles)], axis=1)
    base_rows = jnp.tile(condition, (NOISE, 1)).astype(jnp.float32) + lifted + embedding
    normed = rms_scale(base_rows, norm_gain).astype(jnp.bfloat16)
    row_total = normed.shape[0]
    gate_piece = lax.all_gather(gate_weight, "seq", axis=0, tiled=True)
    up_piece = lax.all_gather(up_weight, "seq", axis=0, tiled=True)
    down_piece = lax.all_gather(down_weight, "seq", axis=0, tiled=True)
    gate_sum = jnp.dot(normed, gate_piece, preferred_element_type=jnp.float32)
    up_sum = jnp.dot(normed, up_piece, preferred_element_type=jnp.float32)
    down_buf = down_piece
    gate_sum, up_sum, down_buf = (gate_sum, up_sum, down_buf)
    hidden = (jax.nn.silu(gate_sum) * up_sum).astype(jnp.bfloat16)
    partial_out = down_product(hidden, down_buf)
    own_count = row_total // lax.axis_size("head")
    summed = lax.psum_scatter(
        partial_out.astype(jnp.bfloat16), "head", scatter_dimension=0, tiled=True
    ).astype(jnp.float32)
    own_base = lax.dynamic_slice_in_dim(base_rows, lax.axis_index("head") * own_count, own_count, 0)
    mixed_rows = own_base + summed
    final_rows = rms_scale(mixed_rows, out_gain).astype(jnp.bfloat16)
    predicted = jnp.dot(final_rows, latent_out, preferred_element_type=jnp.float32)
    draws_here = own_count // slot_count
    predicted = jnp.transpose(
        predicted.reshape(draws_here, slot_count, latent_dim), (1, 0, 2)
    ).reshape(slot_count, draws_here * latent_dim)
    prediction = jnp.where(slot_valid[:, None], predicted, 0.0)
    return (attention_out, grad_queries, grad_keys, grad_values, prediction)


def solution(mesh):
    placed = (
        P("seq", "head"),
        P("seq", "head"),
        P("seq", "head"),
        P("seq", "head"),
        P("seq"),
        P("seq", None),
        P("seq", None),
        P("seq", None),
        P(),
        P(),
        P("seq", "head"),
        P("seq", "head"),
        P("seq", "head"),
        P(),
        P(),
    )
    return jax.shard_map(
        shards,
        mesh=mesh,
        in_specs=placed,
        out_specs=(
            P("seq", "head"),
            P("seq", "head"),
            P("seq", "head"),
            P("seq", "head"),
            P("seq", "head"),
        ),
        check_vma=False,
    )
```

profile of v0, /device:TPU:8, one launch (start us, length us, event | category | flops | bytes accessed | tf_op | source)
XLA Modules:
  0.0 1047.3 jit_solution(8305968204868247405)
XLA Ops:
  13.2 149.6 %all-gather.6.cloned.1.call-done = bf16[4096,128]{1,0:T(8,128)(2,1)} async-done(((bf16[128,128]{1,0:T(8,128)(2,1)}), bf16[4096,128]{1,0:T(8,128)(2,1)}) %all-gather.6.cloned.1.call-update) | async-done | bytes 1048592 | tf_op jit(solution)/shard_map/all_gather | solution.py:172
  162.8 153.0 %all-gather.8.cloned.1.call-done = bf16[4096,128]{1,0:T(8,128)(2,1)} async-done(((bf16[128,128]{1,0:T(8,128)(2,1)}), bf16[4096,128]{1,0:T(8,128)(2,1)}) %all-gather.8.cloned.1.call-update) | async-done | bytes 1048592 | tf_op jit(solution)/shard_map/all_gather | solution.py:173
  315.9 13.8 %while.32 = (s32[]{:T(128)}, f32[1,7,128]{2,1,0:T(8,128)S(1)}, f32[1,7,128]{2,1,0:T(8,128)S(1)}, f32[1,7,128,128]{3,2,1,0:T(8,128)S(1)}, s32[128]{0:T(128)S(1)},...) while((s32[]{:T(128)}, f32[1,7,128]{2,1,0:T(8,128)S(1)}, ...), condition=%wide.region_5.6_spmd, body=%wide.region_0.5_spmd.sunk | while | flops 240225408 | bytes 7238445 | solution.py:64
  317.1 3.7 conditional.4
  317.3 1.3 fusion
  318.7 1.7 fusion.5
  331.0 15.4 %while.33 = (s32[]{:T(128)}, f32[1,7,128,128]{3,2,1,0:T(8,128)S(1)}, bf16[4096,256]{0,1:T(8,128)(2,1)S(1)}, s32[128]{0:T(128)S(1)}, bf16[4096,128]{1,0:T(8,128)(...) while((s32[]{:T(128)}, ...), condition=%wide.region_9.10_spmd, body=%wide.region_6.9_spmd.sunk | while | flops 591249920 | bytes 11415365 | solution.py:128
  332.2 5.2 conditional.5
  332.4 1.4 fusion.26
  336.1 1.4 fusion.28
  346.4 2.5 copy.47
  349.2 6.4 multiply_cosine_fusion
  355.8 8.3 all_gather.20
  364.6 2.6 multiply_reduce_fusion
  367.1 122.3 %all-gather.10.cloned.1.call-done = bf16[3584,1408]{1,0:T(8,128)(2,1)} async-done(((bf16[112,1408]{1,0:T(8,128)(2,1)}), bf16[3584,1408]{1,0:T(8,128)(2,1)}) %all-gather.10.cloned.1.call-update) | async-done | bytes 10092560 | tf_op jit(solution)/shard_map/all_gather | solution.py:236
  489.4 8.1 fusion.58
  497.5 164.8 %all-gather.12.cloned.1.call-done = bf16[3584,1408]{1,0:T(8,128)(2,1)} async-done(((bf16[112,1408]{1,0:T(8,128)(2,1)}), bf16[3584,1408]{1,0:T(8,128)(2,1)}) %all-gather.12.cloned.1.call-update) | async-done | bytes 10092560 | tf_op jit(solution)/shard_map/all_gather | solution.py:237
  662.3 172.4 %all-gather.14.cloned.1.call-done = bf16[3584,1408]{1,0:T(8,128)(2,1)} async-done(((bf16[112,1408]{1,0:T(8,128)(2,1)}), bf16[3584,1408]{1,0:T(8,128)(2,1)}) %all-gather.14.cloned.1.call-update) | async-done | bytes 10092560 | tf_op jit(solution)/shard_map/all_gather | solution.py:238
  834.6 15.0 %convolution_convert_fusion = bf16[256,3584]{1,0:T(8,128)(2,1)} fusion(bf16[3584,1408]{1,0:T(8,128)(2,1)} %all-gather.14.cloned.1.call-done, bf16[3584,1408]{1,0:T(8,128)(2,1)} %all-gather.12.cloned.1.call-done, f32[256,1408]{1,0:T(8,128)S(1)} %fusion.58, f32[256,3584]{1,0:T(8,128)} %get-tuple-element.470, f32[3584]{0:T(1024)S(1)} %copy-done.9, ...), kind=kOutput, calls=%fused_computation.62 | convolution fusion | flops 5173215232 | bytes 27147264 | tf_op jit(solution)/shard_map/dot_general | solution.py:136
  852.9 142.9 %reduce-scatter.3.cloned.1.call-done = bf16[128,256]{1,0:T(8,128)(2,1)} async-done(((bf16[4096,256]{1,0:T(8,128)(2,1)}), bf16[128,256]{1,0:T(8,128)(2,1)}) %reduce-scatter.3.cloned.1.call-update) | async-done | bytes 65552 | tf_op jit(solution)/shard_map/reduce_scatter | solution.py:191
  995.7 1.4 fusion.59
  997.1 39.5 %reduce-scatter.5.cloned.1.call-done = bf16[64,3584]{1,0:T(8,128)(2,1)} async-done(((bf16[256,3584]{1,0:T(8,128)(2,1)}), bf16[64,3584]{1,0:T(8,128)(2,1)}) %reduce-scatter.5.cloned.1.call-update) | async-done | bytes 458768 | tf_op jit(solution)/shard_map/reduce_scatter | solution.py:246
  1036.6 1.5 multiply_reduce_fusion.1
  1038.2 2.3 convolution_select_fusion
  (111 shorter events, 23.6 us)
Async XLA Ops:
  7.2 357.4 %copy-start = (bf16[64,3584]{1,0:T(8,128)(2,1)S(1)}, bf16[64,3584]{1,0:T(8,128)(2,1)}, u32[]{:S(2)}) copy-start(bf16[64,3584]{1,0:T(8,128)(2,1)} %param.31) | copy-start | bytes 1376260
  7.2 4.8 copy-start.3
  7.2 5.0 copy-start.8
  7.2 5.2 copy-start.4
  7.2 5.5 copy-start.5
  7.2 5.5 copy-start.7
  7.2 155.6 %all-gather.6.cloned.1.call-start = ((), (), s32[]{:S(2)}) async-start(), calls=%async_computation.2 | async-start | bytes 1081344 | tf_op jit(solution)/shard_map/all_gather | solution.py:172
  8.0 307.9 %all-gather.8.cloned.1.call-start = ((), (), s32[]{:S(2)}) async-start(), calls=%async_computation.3 | async-start | bytes 1081344 | tf_op jit(solution)/shard_map/all_gather | solution.py:173
  8.7 480.7 %all-gather.10.cloned.1.call-start = ((), (), s32[]{:S(2)}) async-start(), calls=%async_computation.5 | async-start | bytes 10407936 | tf_op jit(solution)/shard_map/all_gather | solution.py:236
  9.5 652.8 %all-gather.12.cloned.1.call-start = ((), (), s32[]{:S(2)}) async-start(), calls=%async_computation.6 | async-start | bytes 10407936 | tf_op jit(solution)/shard_map/all_gather | solution.py:237
  10.0 824.6 %all-gather.14.cloned.1.call-start = ((), (), s32[]{:S(2)}) async-start(), calls=%async_computation.7 | async-start | bytes 10407936 | tf_op jit(solution)/shard_map/all_gather | solution.py:238
  10.6 985.1 %reduce-scatter.3.cloned.1.call-start = ((), (), s32[]{:S(2)}) async-start(), calls=%async_computation.4 | async-start | bytes 2162688 | tf_op jit(solution)/shard_map/reduce_scatter | solution.py:191
  348.9 6.7 copy-start.1
  349.0 687.7 %reduce-scatter.5.cloned.1.call-start = ((), (), s32[]{:S(2)}) async-start(), calls=%async_computation.8 | async-start | bytes 2293760 | tf_op jit(solution)/shard_map/reduce_scatter | solution.py:246
  364.5 124.9 %copy-start.9 = (f32[3584]{0:T(1024)S(1)}, f32[3584]{0:T(1024)}, u32[]{:S(2)}) copy-start(f32[3584]{0:T(1024)} %param.32) | copy-start | bytes 43012
  851.8 186.5 %copy-start.2 = (bf16[3584,64]{0,1:T(8,128)(2,1)S(1)}, bf16[3584,64]{0,1:T(8,128)(2,1)}, u32[]{:S(2)}) copy-start(bf16[3584,64]{0,1:T(8,128)(2,1)} %param.37) | copy-start | bytes 1376260
  851.8 186.5 %copy-start.6 = (f32[3584]{0:T(1024)S(1)}, f32[3584]{0:T(1024)}, u32[]{:S(2)}) copy-start(f32[3584]{0:T(1024)} %param.36) | copy-start | bytes 43012
Sparse Core Ops, SparseCore 0:
  9.7 153.0 all-gather.5
  164.5 151.2 all-gather.7
  317.5 171.9 all-gather.9
  490.9 171.2 all-gather.11
  663.7 170.8 all-gather.13
  836.9 158.8 reduce-scatter.2
  998.6 38.0 reduce-scatter.4
where the time goes:
time: 1050 us
  waiting for transfers between devices  948 us (90%)
  matrix products  36.1 us (3%)
  local copies, waits for them, and re-layouts  18.1 us (2%)
  between operations  14.4 us (1%)
  other arithmetic  11.2 us (1%)
  loops' own time  11.2 us (1%)
    all_gather x1, waiting for transfers between devices, shards(): down_piece = lax.all_gather(down_weight, 'seq', axis=0, tiled=True)  172 us
    all_gather x1, waiting for transfers between devices, shards(): up_piece = lax.all_gather(up_weight, 'seq', axis=0, tiled=True)  165 us
    all_gather x1, waiting for transfers between devices, shards(): lax.all_gather(value_vectors, 'seq', axis=0, tiled=True)  153 us
    all_gather x1, waiting for transfers between devices, shards(): lax.all_gather(key_vectors, 'seq', axis=0, tiled=True)  150 us
    reduce_scatter x1, waiting for transfers between devices, shards(): lax.psum_scatter(all_terms.astype(jnp.bfloat16), 'seq', scatter_dimension...  143 us
    all_gather x1, waiting for transfers between devices, shards(): gate_piece = lax.all_gather(gate_weight, 'seq', axis=0, tiled=True)  122 us
    reduce_scatter x1, waiting for transfers between devices, shards(): lax.psum_scatter(partial_out.astype(jnp.bfloat16), 'head', scatter_dimens...  39.5 us
  transfers between devices with their start and end apart: 7, of which 7 were waited for; matrix products, arithmetic and copies ran while one was open for 6% of the time, Pallas kernels for 0%

commit v1 on v0

v1 whole, which is shorter than its diff:
```python
import math

import jax
import jax.numpy as jnp
import numpy as np
from jax import lax
from jax.experimental import pallas as pl
from jax.experimental.pallas import tpu as pltpu
from jax.sharding import PartitionSpec as P

MESH = pl.DeviceIdType.MESH
F32 = jnp.float32
BF16 = jnp.bfloat16

HD = 128
GRP = 7
TOK = 128
ROWS = GRP * TOK
D = 3584
HALF = D // 2
LAT = 64
CAP = 64
NOISE = 4
N_SEQ = 32
N_HEAD = 4
FEAT = 112
GUW = 1408
DNW = 768
MAIN = 640
KC = 256
HEADW = D // N_HEAD
SCALE = 1.0 / math.sqrt(HD)
LOG2E = math.log2(math.e)
NEG = -1e30

HALVES = {"kv": ((0, 128), (128, 128)), "gu": ((0, 64), (64, 48)), "dn": ((0, 64), (64, 48))}


def contract_rows(left, right):
    return lax.dot_general(left, right, (((0,), (0,)), ((), ())), preferred_element_type=F32)


def dot(left, right):
    return jnp.dot(left, right, preferred_element_type=F32)


def kernel(
    q_ref, k_ref, v_ref, do_ref, mask_ref, clean_ref, noise_ref, time_ref, lin_ref, ngain_ref,
    gate_ref, up_ref, down_ref, ogain_ref, lout_ref, freq_ref,
    out_ref, dq_ref, dk_ref, dv_ref, pred_ref,
    kv, gu, dn, sgu, sdn, qs, qt, dos, dot_t, probs, acc_t, dkv, drecv, cond, nz, tm, tab, oha, ohb,
    le, nm, acc, hid, rbuf,
    ssem, rsem, dssem, drsem, fssem, frsem, cssem, crsem,
):
    s = lax.axis_index("seq")
    h = lax.axis_index("head")
    xl = lax.div(s, 16)
    zy = lax.rem(s, 16)
    z = lax.div(zy, 4)
    y = lax.rem(zy, 4)
    mate = (1 - xl) * 16 + zy

    bufs = {"kv": kv, "gu": gu, "dn": dn}
    sent = []
    recv_at = {}

    def recv_slot(key):
        if key not in recv_at:
            recv_at[key] = len(recv_at)
        return rsem.at[recv_at[key]]

    def start(src, dst, key, dev):
        copy = pltpu.make_async_remote_copy(
            src_ref=src, dst_ref=dst, send_sem=ssem.at[len(sent)], recv_sem=recv_slot(key),
            device_id=dev, device_id_type=MESH,
        )
        copy.start()
        sent.append(copy)

    def landed(dst, key, dev):
        pltpu.make_async_remote_copy(
            src_ref=dst, dst_ref=dst, send_sem=ssem.at[0], recv_sem=recv_slot(key),
            device_id=dev, device_id_type=MESH,
        ).wait_recv()

    def back(pos, dist):
        return lax.rem(pos + 4 - dist, 4)

    def chunk(p, r, d1, d2, half):
        dy, dz = (d1, d2) if r == 0 else (d2, d1)
        view = bufs[p].at[r, back(z, dz) * 4 + back(y, dy)]
        if half is None:
            return view
        first, count = HALVES[p][half]
        return view.at[pl.ds(first, count)]

    def neighbour(r, axis, step):
        along_y = (axis == 1) == (r == 0)
        if along_y:
            return (xl * 16 + z * 4 + back(y, -step), h)
        return (xl * 16 + back(z, -step) * 4 + y, h)

    def send(p, r, d1, d2, axis, step, half=None):
        ref = chunk(p, r, d1, d2, half)
        e1 = (d1 + step) % 4 if axis == 1 else d1
        e2 = (d2 + step) % 4 if axis == 2 else d2
        start(ref, ref, (p, r, e1, e2, half), neighbour(r, axis, step))

    def wait(p, r, d1, d2, half=None):
        landed(chunk(p, r, d1, d2, half), (p, r, d1, d2, half), (mate, h))

    def p1_send(p, r):
        send(p, r, 0, 0, 1, 1)
        send(p, r, 0, 0, 1, -1)

    def p1_fwd(p, r):
        wait(p, r, 1, 0)
        send(p, r, 1, 0, 1, 1, 0)
        wait(p, r, 3, 0)
        send(p, r, 3, 0, 1, -1, 1)

    def p1_fin(p, r):
        wait(p, r, 2, 0, 0)
        wait(p, r, 2, 0, 1)

    def p2_send(p, r, d1):
        send(p, r, d1, 0, 2, 1)
        send(p, r, d1, 0, 2, -1)

    def p2_fwd(p, r, d1):
        wait(p, r, d1, 1)
        send(p, r, d1, 1, 2, 1, d1 % 2)
        wait(p, r, d1, 3)
        send(p, r, d1, 3, 2, -1, 1 - d1 % 2)

    def p2_fin(p, r, d1):
        wait(p, r, d1, 2, 0)
        wait(p, r, d1, 2, 1)

    def both(step, p, *rest):
        step(p, 0, *rest)
        step(p, 1, *rest)

    barrier = pltpu.get_barrier_semaphore()

    def greet(i, carry):
        other = lax.rem(s + i, N_SEQ)
        pl.semaphore_signal(barrier, inc=1, device_id=(other, h), device_id_type=MESH)
        return carry

    lax.fori_loop(1, N_SEQ, greet, 0)
    line = [(dx, dh) for dx in (0, 1) for dh in range(N_HEAD) if (dx, dh) != (0, 0)]

    def on_line(dx, dh):
        ox = lax.rem(xl + dx, 2)
        oh = lax.rem(h + dh, N_HEAD)
        return ox, oh, (ox * 16 + zy, oh)

    for dx, dh in line:
        if dh:
            pl.semaphore_signal(barrier, inc=1, device_id=on_line(dx, dh)[2], device_id_type=MESH)
    pl.semaphore_wait(barrier, N_SEQ - 1 + 6)

    kv[xl, zy, 0:TOK, :] = k_ref[...]
    kv[xl, zy, TOK : 2 * TOK, :] = v_ref[...]
    start(kv.at[xl, zy], kv.at[xl, zy], "xkv", (mate, h))

    low = lax.broadcasted_iota(jnp.int32, (FEAT, 128), 1) < 64

    def pack(f, put_gu, put_dn):
        at = f * 768
        mid_gate = gate_ref[:, MAIN : MAIN + 128].astype(F32)
        mid_up = up_ref[:, MAIN : MAIN + 128].astype(F32)
        if f == 0:
            mixed = jnp.where(low, mid_gate, pltpu.roll(mid_up, 64, 1))
        else:
            mixed = jnp.where(low, pltpu.roll(mid_gate, 64, 1), mid_up)
        put_gu(0, gate_ref[:, at : at + MAIN])
        put_gu(MAIN, up_ref[:, at : at + MAIN])
        put_gu(2 * MAIN, mixed.astype(BF16))
        put_dn(down_ref[:, f * MAIN : f * MAIN + DNW])

    def own_gu(at, value):
        gu[xl, zy, :, at : at + value.shape[1]] = value

    def own_dn(value):
        dn[xl, zy] = value

    def mate_gu(at, value):
        sgu[:, at : at + value.shape[1]] = value

    def mate_dn(value):
        sdn[...] = value

    for f in (0, 1):

        @pl.when(xl == f)
        def _():
            pack(1 - f, mate_gu, mate_dn)
            pack(f, own_gu, own_dn)

    start(sgu, gu.at[xl, zy], "xgu", (mate, h))

    share = jnp.cos((time_ref[...].astype(F32) / 1000.0 + 0.008) / 1.008 * (math.pi / 2.0)) ** 2
    signal, noise_part = jnp.sqrt(share), jnp.sqrt(1.0 - share)
    nz[xl] = jnp.zeros((NOISE * CAP, 128), BF16)
    tm[xl] = jnp.zeros((CAP, 128), jnp.int32)
    tm[xl, :, 0:NOISE] = time_ref[...]
    for n in range(NOISE):
        row = signal[:, n : n + 1] * clean_ref[...] + noise_part[:, n : n + 1] * noise_ref[:, n * LAT : (n + 1) * LAT]
        nz[xl, n * CAP : (n + 1) * CAP, 0:LAT] = row.astype(BF16)
    start(nz.at[xl], nz.at[xl], "xnz", (mate, h))
    start(tm.at[xl], tm.at[xl], "xtm", (mate, h))

    landed(kv.at[1 - xl, zy], "xkv", (mate, h))
    both(p1_send, "kv")
    both(p2_send, "kv", 0)
    start(sdn, dn.at[xl, zy], "xdn", (mate, h))

    for j in range(GRP):
        cols = slice(j * HD, (j + 1) * HD)
        qs[cols, :] = q_ref[:, cols]
        dos[cols, :] = do_ref[:, cols]
        qt[:, cols] = q_ref[:, cols].astype(F32).T.astype(BF16)
        dot_t[:, cols] = do_ref[:, cols].astype(F32).T.astype(BF16)

    both(p1_fwd, "kv")
    both(p2_send, "kv", 1)
    both(p2_send, "kv", 3)
    landed(gu.at[1 - xl, zy], "xgu", (mate, h))
    both(p1_send, "gu")

    steps = lax.broadcasted_iota(jnp.int32, (32, HALF), 0).astype(F32)
    for k, mult in ((0, 32.0), (2, 1.0)):
        angle = (steps * mult) * freq_ref[...]
        for kk, value in ((k, jnp.cos(angle)), (k + 1, jnp.sin(angle))):
            high = value.astype(BF16)
            rest = value - high.astype(F32)
            middle = rest.astype(BF16)
            tab[kk, 0:32, :] = high
            tab[kk, 32:64, :] = middle
            tab[kk, 64:96, :] = (rest - middle.astype(F32)).astype(BF16)
            tab[kk, 96:128, :] = jnp.zeros((32, HALF), BF16)

    both(p1_fin, "kv")
    both(p2_send, "kv", 2)
    for d in (0, 1, 3, 2):
        both(p2_fwd, "kv", d)
    both(p1_fwd, "gu")
    both(p2_send, "gu", 0)

    landed(nz.at[1 - xl], "xnz", (mate, h))
    landed(tm.at[1 - xl], "xtm", (mate, h))
    lane = lax.broadcasted_iota(jnp.int32, (CAP, 128), 1)
    for b in (0, 1):
        for n in range(NOISE):
            rows = slice((b * NOISE + n) * CAP, (b * NOISE + n + 1) * CAP)
            step = tm[b, :, n : n + 1]
            for ref, digit in ((oha, step >> 5), (ohb, step & 31)):
                ref[rows, :] = jnp.where((lane & 31) == digit, jnp.where(lane < 96, 1.0, 0.0), 0.0).astype(BF16)

    both(p2_send, "gu", 1)
    both(p2_send, "gu", 3)

    def embed(j, carry):
        c0 = pl.ds(pl.multiple_of(j * 256, 256), 256)
        c1 = pl.ds(pl.multiple_of(HALF + j * 256, 256), 256)
        noisy = nz[...].reshape(2 * NOISE * CAP, 128)[:, 0:LAT]
        ca, sa = dot(oha[...], tab[0, :, c0]), dot(oha[...], tab[1, :, c0])
        cb, sb = dot(ohb[...], tab[2, :, c0]), dot(ohb[...], tab[3, :, c0])
        le[:, c0] = ca * cb - sa * sb + dot(noisy, lin_ref[:, c0])
        le[:, c1] = sa * cb + ca * sb + dot(noisy, lin_ref[:, c1])
        return carry

    lax.fori_loop(0, HALF // 256, embed, 0)

    for d in (0, 1, 3, 2):
        both(p2_fin, "kv", d)
    both(p1_fin, "gu")
    both(p2_send, "gu", 2)
    landed(dn.at[1 - xl, zy], "xdn", (mate, h))
    both(p1_send, "dn")

    n_steps = lax.div(s, 2) + 1

    def keys_of(c):
        blocks = kv.at[lax.div(c, 8), pl.ds(lax.rem(c, 8) * 2, 2)]
        return blocks[:, 0:TOK, :].reshape(KC, HD), blocks[:, TOK : 2 * TOK, :].reshape(KC, HD)

    def scores_of(c, masked):
        score = dot(keys_of(c)[0], qt[...]) * (SCALE * LOG2E)
        if masked:
            key_pos = c * KC + lax.broadcasted_iota(jnp.int32, (KC, ROWS), 0)
            query_pos = s * TOK + (lax.broadcasted_iota(jnp.int32, (KC, ROWS), 1) & (TOK - 1))
            score = jnp.where(key_pos <= query_pos, score, NEG)
        return score

    def fold(values, reduce):
        return reduce(values.reshape(KC // 8, 8, ROWS), axis=0)

    def max_step(c, run, masked=False):
        return jnp.maximum(run, fold(scores_of(c, masked), jnp.max))

    row_max = lax.fori_loop(0, n_steps - 1, max_step, jnp.full((8, ROWS), NEG, F32))
    row_max = max_step(n_steps - 1, row_max, True)
    row_max = jnp.max(row_max, axis=0, keepdims=True)
    both(p2_fwd, "gu", 0)

    acc_t[...] = jnp.zeros_like(acc_t)

    def sum_step(c, run, masked=False):
        soft = jnp.exp2(scores_of(c, masked) - row_max)
        soft_b = soft.astype(BF16)
        probs[pl.ds(pl.multiple_of(c * KC, KC), KC), :] = soft_b
        acc_t[...] += contract_rows(keys_of(c)[1], soft_b)
        return run + fold(soft, jnp.sum)

    total = lax.fori_loop(0, n_steps - 1, sum_step, jnp.zeros((8, ROWS), F32))
    total = sum_step(n_steps - 1, total, True)
    total = jnp.sum(total, axis=0, keepdims=True)
    inverse = 1.0 / total
    out_t = (acc_t[...] / total).astype(BF16)
    delta = jnp.sum(out_t.astype(F32) * dot_t[...].astype(F32), axis=0, keepdims=True)
    for j in range(GRP):
        cols = slice(j * HD, (j + 1) * HD)
        out_ref[:, cols] = out_t[:, cols].astype(F32).T.astype(BF16)

    mask = mask_ref[...]
    ones = jnp.broadcast_to(mask.astype(F32), (8, TOK)).astype(BF16)
    before = lax.broadcasted_iota(jnp.int32, (TOK, TOK), 0) <= lax.broadcasted_iota(jnp.int32, (TOK, TOK), 1)
    rank = dot(ones, jnp.where(before, 1.0, 0.0).astype(BF16))[0:1, :] - 1.0
    slot = lax.broadcasted_iota(jnp.int32, (CAP, TOK), 0).astype(F32)
    chosen = jnp.where(rank == slot, jnp.where(mask == 1, 1.0, 0.0), 0.0)
    valid = jnp.sum(chosen, axis=1, keepdims=True) > 0.5
    cond[xl, h] = dot(chosen.astype(BF16), out_ref[...]).astype(BF16)
    cond_sent = []
    for i, (dx, dh) in enumerate(line):
        copy = pltpu.make_async_remote_copy(
            src_ref=cond.at[xl, h], dst_ref=cond.at[xl, h], send_sem=cssem.at[i],
            recv_sem=crsem.at[xl * N_HEAD + h], device_id=on_line(dx, dh)[2], device_id_type=MESH,
        )
        copy.start()
        cond_sent.append(copy)

    both(p2_fwd, "gu", 1)
    both(p1_fwd, "dn")
    both(p2_send, "dn", 0)

    acc_t[...] = jnp.zeros_like(acc_t)

    def term_copy(kb):
        return pltpu.make_async_remote_copy(
            src_ref=dkv.at[kb], dst_ref=drecv.at[s], send_sem=dssem.at[kb], recv_sem=drsem.at[s],
            device_id=(kb, h), device_id_type=MESH,
        )

    def grad_step(c, carry):
        keys, values = keys_of(c)
        prob = probs[pl.ds(pl.multiple_of(c * KC, KC), KC), :].astype(F32) * inverse
        ds = (prob * (dot(values, dot_t[...]) - delta)).astype(BF16)
        acc_t[...] += contract_rows(keys, ds)
        dkv[pl.ds(2 * c, 2), 0:TOK, :] = (dot(ds, qs[...]) * SCALE).astype(BF16).reshape(2, TOK, HD)
        dkv[pl.ds(2 * c, 2), TOK : 2 * TOK, :] = dot(prob.astype(BF16), dos[...]).astype(BF16).reshape(2, TOK, HD)
        for i in (0, 1):

            @pl.when(2 * c + i < s)
            def _():
                term_copy(2 * c + i).start()

        return carry

    for part in range(4):
        lax.fori_loop(part * 4, jnp.minimum(n_steps, part * 4 + 4), grad_step, 0)
        if part == 0:
            both(p2_fwd, "gu", 3)
            both(p2_send, "dn", 1)
            both(p2_send, "dn", 3)
        elif part == 1:
            both(p2_fwd, "gu", 2)
            both(p1_fin, "dn")
            both(p2_send, "dn", 2)
        elif part == 2:
            both(p2_fwd, "dn", 0)

    for j in range(GRP):
        cols = slice(j * HD, (j + 1) * HD)
        dq_ref[:, cols] = (acc_t[:, cols] * SCALE).T.astype(BF16)

    for dx, dh in line:
        ox, oh, dev = on_line(dx, dh)
        pltpu.make_async_remote_copy(
            src_ref=cond.at[ox, oh], dst_ref=cond.at[ox, oh], send_sem=cssem.at[0],
            recv_sem=crsem.at[ox * N_HEAD + oh], device_id=dev, device_id_type=MESH,
        ).wait_recv()

    def norm_rows(g, carry):
        rows = pl.ds(pl.multiple_of(g * CAP, CAP), CAP)
        square = jnp.zeros((CAP, 1), F32)
        for hh in range(N_HEAD):
            cols = slice(hh * HEADW, (hh + 1) * HEADW)
            base = le[rows, cols] + cond[lax.div(g, NOISE), hh].astype(F32)
            le[rows, cols] = base
            square += jnp.sum(base * base, axis=1, keepdims=True)
        scale = lax.rsqrt(square * (1.0 / D) + 1e-06)
        for hh in range(N_HEAD):
            cols = slice(hh * HEADW, (hh + 1) * HEADW)
            nm[rows, cols] = (le[rows, cols] * scale * ngain_ref[:, cols]).astype(BF16)
        return carry

    lax.fori_loop(0, 2 * NOISE, norm_rows, 0)
    both(p2_fwd, "dn", 1)
    for d in (0, 1, 3, 2):
        both(p2_fin, "gu", d)

    for k in range(4):
        piece = gu[k // 2, (k % 2) * 8 : (k % 2) * 8 + 8].reshape(8 * FEAT, GUW)
        part = dot(nm[:, k * 896 : (k + 1) * 896], piece)
        if k == 0:
            acc[...] = part
        else:
            acc[...] += part
        if k == 1:
            both(p2_fwd, "dn", 3)

    def silu(value):
        return value / (1.0 + jnp.exp(-value))

    both(p2_fwd, "dn", 2)
    mixed = acc[:, 2 * MAIN :]
    turned = pltpu.roll(mixed, 64, 1)
    lower_half = lax.broadcasted_iota(jnp.int32, (2 * NOISE * CAP, 128), 1) < 64

    @pl.when(xl == 0)
    def _():
        hid[:, 0:MAIN] = (silu(acc[:, 0:MAIN]) * acc[:, MAIN : 2 * MAIN]).astype(BF16)
        hid[:, MAIN:DNW] = jnp.where(lower_half, silu(mixed) * turned, 0.0).astype(BF16)

    @pl.when(xl == 1)
    def _():
        hid[:, 128:DNW] = (silu(acc[:, 0:MAIN]) * acc[:, MAIN : 2 * MAIN]).astype(BF16)
        hid[:, 0:128] = jnp.where(lower_half, 0.0, silu(turned) * mixed).astype(BF16)

    for d in (0, 1, 3, 2):
        both(p2_fin, "dn", d)

    part_sent = []
    for k in range(4):
        cols = slice(k * 896, (k + 1) * 896)
        piece = dn[k // 2, (k % 2) * 8 : (k % 2) * 8 + 8].reshape(8 * FEAT, DNW)
        part = lax.dot_general(hid[...], piece, (((1,), (1,)), ((), ())), preferred_element_type=F32)
        nm[:, cols] = part.astype(BF16)
        for i, (dx, dh) in enumerate(line):
            ox, oh, dev = on_line(dx, dh)
            rows = pl.ds(pl.multiple_of((ox * NOISE + oh) * CAP, CAP), CAP)
            me = xl * N_HEAD + h
            copy = pltpu.make_async_remote_copy(
                src_ref=nm.at[rows, cols], dst_ref=rbuf.at[me, k], send_sem=fssem.at[k * 7 + i],
                recv_sem=frsem.at[me * 4 + k], device_id=dev, device_id_type=MESH,
            )
            copy.start()
            part_sent.append(copy)

    def add_terms(i, run):
        pltpu.make_async_remote_copy(
            src_ref=drecv.at[i], dst_ref=drecv.at[i], send_sem=dssem.at[0], recv_sem=drsem.at[i],
            device_id=(mate, h), device_id_type=MESH,
        ).wait_recv()
        return run + drecv[i].astype(F32)

    terms = lax.fori_loop(s + 1, N_SEQ, add_terms, dkv[s].astype(F32))
    dk_ref[...] = terms[0:TOK].astype(BF16)
    dv_ref[...] = terms[TOK : 2 * TOK].astype(BF16)

    own = pl.ds(pl.multiple_of((xl * NOISE + h) * CAP, CAP), CAP)
    square = jnp.zeros((CAP, 1), F32)
    for k in range(4):
        cols = slice(k * 896, (k + 1) * 896)
        rows = le[own, cols] + nm[own, cols].astype(F32)
        for dx, dh in line:
            ox, oh, dev = on_line(dx, dh)
            src = ox * N_HEAD + oh
            pltpu.make_async_remote_copy(
                src_ref=rbuf.at[src, k], dst_ref=rbuf.at[src, k], send_sem=fssem.at[0],
                recv_sem=frsem.at[src * 4 + k], device_id=dev, device_id_type=MESH,
            ).wait_recv()
            rows += rbuf[src, k].astype(F32)
        le[own, cols] = rows
        square += jnp.sum(rows * rows, axis=1, keepdims=True)
    scale = lax.rsqrt(square * (1.0 / D) + 1e-06)
    result = jnp.zeros((CAP, LAT), F32)
    for k in range(4):
        cols = slice(k * 896, (k + 1) * 896)
        final = (le[own, cols] * scale * ogain_ref[:, cols]).astype(BF16)
        result += dot(final, lout_ref[cols, :])
    pred_ref[...] = jnp.where(valid, result, 0.0)

    for copy in sent + cond_sent + part_sent:
        copy.wait_send()

    def term_left(kb, carry):
        term_copy(kb).wait_send()
        return carry

    lax.fori_loop(0, s, term_left, 0)


def shards(
    queries, key_vectors, value_vectors, out_cotangent, latent_mask, clean_latents, noise_draws, timesteps,
    latent_in, norm_gain, gate_weight, up_weight, down_weight, out_gain, latent_out,
):
    frequencies = np.exp(-math.log(10000.0) * np.arange(HALF, dtype=np.float32) / HALF).astype(np.float32)
    vmem = pl.BlockSpec(memory_space=pltpu.VMEM)
    dma = pltpu.SemaphoreType.DMA
    n_sems = 140
    return pl.pallas_call(
        kernel,
        out_shape=(
            jax.ShapeDtypeStruct((TOK, ROWS), BF16),
            jax.ShapeDtypeStruct((TOK, ROWS), BF16),
            jax.ShapeDtypeStruct((TOK, HD), BF16),
            jax.ShapeDtypeStruct((TOK, HD), BF16),
            jax.ShapeDtypeStruct((CAP, LAT), F32),
        ),
        in_specs=[vmem] * 16,
        out_specs=(vmem,) * 5,
        scratch_shapes=[
            pltpu.VMEM((2, 16, 2 * TOK, HD), BF16),
            pltpu.VMEM((2, 16, FEAT, GUW), BF16),
            pltpu.VMEM((2, 16, FEAT, DNW), BF16),
            pltpu.VMEM((FEAT, GUW), BF16),
            pltpu.VMEM((FEAT, DNW), BF16),
            pltpu.VMEM((ROWS, HD), BF16),
            pltpu.VMEM((HD, ROWS), BF16),
            pltpu.VMEM((ROWS, HD), BF16),
            pltpu.VMEM((HD, ROWS), BF16),
            pltpu.VMEM((N_SEQ * TOK, ROWS), BF16),
            pltpu.VMEM((HD, ROWS), F32),
            pltpu.VMEM((N_SEQ, 2 * TOK, HD), BF16),
            pltpu.VMEM((N_SEQ, 2 * TOK, HD), BF16),
            pltpu.VMEM((2, N_HEAD, CAP, HEADW), BF16),
            pltpu.VMEM((2, NOISE * CAP, 128), BF16),
            pltpu.VMEM((2, CAP, 128), jnp.int32),
            pltpu.VMEM((4, 128, HALF), BF16),
            pltpu.VMEM((2 * NOISE * CAP, 128), BF16),
            pltpu.VMEM((2 * NOISE * CAP, 128), BF16),
            pltpu.VMEM((2 * NOISE * CAP, D), F32),
            pltpu.VMEM((2 * NOISE * CAP, D), BF16),
            pltpu.VMEM((2 * NOISE * CAP, GUW), F32),
            pltpu.VMEM((2 * NOISE * CAP, DNW), BF16),
            pltpu.VMEM((8, 4, CAP, 896), BF16),
            dma((n_sems,)),
            dma((n_sems,)),
            dma((N_SEQ,)),
            dma((N_SEQ,)),
            dma((28,)),
            dma((32,)),
            dma((7,)),
            dma((8,)),
        ],
        compiler_params=pltpu.CompilerParams(
            collective_id=0, has_side_effects=True, vmem_limit_bytes=63 * 1024 * 1024
        ),
    )(
        queries, key_vectors, value_vectors, out_cotangent, latent_mask.reshape(1, TOK), clean_latents, noise_draws,
        timesteps, latent_in, norm_gain.reshape(1, D), gate_weight, up_weight, down_weight, out_gain.reshape(1, D),
        latent_out, jnp.asarray(frequencies.reshape(1, HALF)),
    )


def solution(mesh):
    placed = (
        P("seq", "head"),
        P("seq", "head"),
        P("seq", "head"),
        P("seq", "head"),
        P("seq"),
        P("seq", None),
        P("seq", None),
        P("seq", None),
        P(),
        P(),
        P("seq", "head"),
        P("seq", "head"),
        P("seq", "head"),
        P(),
        P(),
    )
    return jax.shard_map(
        shards,
        mesh=mesh,
        in_specs=placed,
        out_specs=(P("seq", "head"),) * 5,
        check_vma=False,
    )
```

time: 1050 us -> 184 us (0.18)
  waiting for transfers between devices: 948 us -> 0 us
  Pallas kernels: 0 us -> 170 us
  matrix products: 36.1 us -> 0 us
  between operations: 14.4 us -> 0.67 us
  other arithmetic: 11.2 us -> 0 us
  loops' own time: 11.2 us -> 0 us
    all_gather x5 -> x0, waiting for transfers between devices: 762 us -> none  [the longest x1 172 us: shards(): down_piece = lax.all_gather(down_weight, 'seq', axis=0, tiled=True)]
    reduce_scatter x2 -> x0, waiting for transfers between devices: 182 us -> none  [the longest x1 143 us: shards(): lax.psum_scatter(all_terms.astype(jnp.bfloat16), 'seq', scatter_dimension...]
    pallas_call x0 -> x1, Pallas kernels: none -> 170 us  [shards(): pl.pallas_call(kernel, out_shape=(jax.ShapeDtypeStruct((TOK, ROWS), BF16)...]
    dot_general x12 -> x0, matrix products: 36.1 us -> none  [the longest x1 15 us: down_product(): lax.dot_general(hidden, down_rows, (((1,), (1,)), ((), ())), preferred_el...]
    another operation x18 -> x0, loops' own time: 11.2 us -> none  [the longest x1 5.44 us: attend_piece(): lax.fori_loop(0, row_count // block_rows, attend_advance, softmax_state)]
    slice x17 -> x0, local copies, waits for them, and re-layouts: 10.7 us -> none  [the longest x8 4.65 us: attend_advance(): query_pos[-1]]
  transfers between devices with their start and end apart: 7 -> 0, of which waited for: 7 -> 0; matrix products, arithmetic and copies ran while one was open for 6% -> 0% of each run, Pallas kernels for 0% -> 0%
where the time goes in v1:
time: 184 us; the launch traced here: 180 us
  Pallas kernels  170 us (92%)
  local copies, waits for them, and re-layouts  9.61 us (5%)
    pallas_call x1, Pallas kernels, shards(): pl.pallas_call(kernel, out_shape=(jax.ShapeDtypeStruct((TOK, ROWS), BF16)...  170 us
    unnamed x19, local copies, waits for them, and re-layouts  7.67 us

profile of v1, /device:TPU:8, one launch (start us, length us, event | category | flops | bytes accessed | tf_op | source)
XLA Modules:
  0.0 180.4 jit_solution(3434662893526733921)
XLA Ops:
  0.6 0.0 copy-start.4
  0.6 1.3 reshape.20.ngain_ref
  2.0 0.0 copy-done.4
  2.0 0.0 copy-start.5
  2.0 0.6 reshape.21.ogain_ref
  2.6 0.1 copy-done.5
  2.7 0.7 copy.21.time_ref
  3.4 2.3 %copy.22.lout_ref = bf16[3584,64]{1,0:T(8,128)(2,1)} copy(bf16[3584,64]{0,1:T(8,128)(2,1)} %param.30) | data formatting | bytes 917504 | tf_op args[14]
  5.7 170.1 %shard_map.191 = (bf16[128,896]{1,0:T(8,128)(2,1)}, bf16[128,896]{1,0:T(8,128)(2,1)}, bf16[128,128]{1,0:T(8,128)(2,1)}, bf16[128,128]{1,0:T(8,128)(2,1)}, f32[64,64]{1,0:T(8,128)}) custom-call(bf16[128,896]{1,0:T(8,128)(2,1)} %q_ref.1, bf16[128,128]{1,0:T(8,128)(2,1)} %k_ref.1, bf16[128,128]{1,0:T(8,128)(2,1)} %v_ref.1, bf16[128,896]{1,0:T(8,128)(2,1)} %do_ref.1, ...), custom_call_target="tpu_custom_call" | custom-call | tf_op jit(solution)/shard_map/pallas_call | solution.py:515
  175.7 0.0 copy-start
  175.8 1.7 copy.28
  177.4 0.0 copy-done
  177.4 0.0 copy-start.3
  177.4 0.7 copy.29
  178.1 0.1 copy-done.3
  178.2 0.0 copy-start.2
  178.2 0.6 copy.30
  178.8 0.2 copy-done.2
  179.0 0.0 copy-start.1
  179.0 0.6 copy.31
  179.6 0.2 copy-done.1
  179.7 0.6 copy.32
Async XLA Ops:
  0.6 1.3 copy-start.4
  2.0 0.7 copy-start.5
  175.7 1.7 copy-start
  177.4 0.8 copy-start.3
  178.2 0.8 copy-start.2
  179.0 0.8 copy-start.1

commit v2 on v1

--- a/solution.py
+++ b/solution.py
@@ -49,46 +49,49 @@
     gate_ref, up_ref, down_ref, ogain_ref, lout_ref, freq_ref,
     out_ref, dq_ref, dk_ref, dv_ref, pred_ref,
     kv, gu, dn, sgu, sdn, qs, qt, dos, dot_t, probs, acc_t, dkv, drecv, cond, nz, tm, tab, oha, ohb,
-    le, nm, acc, hid, rbuf,
-    ssem, rsem, dssem, drsem, fssem, frsem, cssem, crsem,
+    le, nm, acc, hid, s1, s23, r1, r2, r3, fin, xterm,
+    ssem, rsem, dssem, drsem, cssem, crsem,
 ):
     s = lax.axis_index("seq")
     h = lax.axis_index("head")
     xl = lax.div(s, 16)
     zy = lax.rem(s, 16)
+    core = lax.rem(h, 2)
+    x = lax.div(h, 2) * 2 + xl
     z = lax.div(zy, 4)
     y = lax.rem(zy, 4)
     mate = (1 - xl) * 16 + zy
 
     bufs = {"kv": kv, "gu": gu, "dn": dn}
-    sent = []
-    recv_at = {}
-
-    def recv_slot(key):
-        if key not in recv_at:
-            recv_at[key] = len(recv_at)
-        return rsem.at[recv_at[key]]
-
-    def start(src, dst, key, dev):
-        copy = pltpu.make_async_remote_copy(
-            src_ref=src, dst_ref=dst, send_sem=ssem.at[len(sent)], recv_sem=recv_slot(key),
-            device_id=dev, device_id_type=MESH,
+    sem_at = {}
+    leaving = {}
+
+    def copy_of(src, dst, key, dev):
+        at = sem_at.setdefault(key, len(sem_at))
+        return pltpu.make_async_remote_copy(
+            src_ref=src, dst_ref=dst, send_sem=ssem.at[at], recv_sem=rsem.at[at], device_id=dev, device_id_type=MESH
         )
-        copy.start()
-        sent.append(copy)
+
+    def start(make, key):
+        src, dst, dev = make()
+        copy_of(src, dst, key, dev).start()
+        leaving[key] = make
 
     def landed(dst, key, dev):
-        pltpu.make_async_remote_copy(
-            src_ref=dst, dst_ref=dst, send_sem=ssem.at[0], recv_sem=recv_slot(key),
-            device_id=dev, device_id_type=MESH,
-        ).wait_recv()
+        copy_of(dst, dst, key, dev).wait_recv()
+
+    def all_left():
+        for key, make in leaving.items():
+            src, dst, dev = make()
+            copy_of(src, dst, key, dev).wait_send()
 
     def back(pos, dist):
         return lax.rem(pos + 4 - dist, 4)
 
     def chunk(p, r, d1, d2, half):
         dy, dz = (d1, d2) if r == 0 else (d2, d1)
-        view = bufs[p].at[r, back(z, dz) * 4 + back(y, dy)]
+        pz, py = back(z, dz), back(y, dy)
+        view = bufs[p].at[r, py * 4 + pz if p == "dn" and r == 0 else pz * 4 + py]
         if half is None:
             return view
         first, count = HALVES[p][half]
@@ -101,10 +104,14 @@
         return (xl * 16 + back(z, -step) * 4 + y, h)
 
     def send(p, r, d1, d2, axis, step, half=None):
-        ref = chunk(p, r, d1, d2, half)
         e1 = (d1 + step) % 4 if axis == 1 else d1
         e2 = (d2 + step) % 4 if axis == 2 else d2
-        start(ref, ref, (p, r, e1, e2, half), neighbour(r, axis, step))
+
+        def make():
+            ref = chunk(p, r, d1, d2, half)
+            return ref, ref, neighbour(r, axis, step)
+
+        start(make, (p, r, e1, e2, half))
 
     def wait(p, r, d1, d2, half=None):
         landed(chunk(p, r, d1, d2, half), (p, r, d1, d2, half), (mate, h))
@@ -112,6 +119,14 @@
     def p1_send(p, r):
         send(p, r, 0, 0, 1, 1)
         send(p, r, 0, 0, 1, -1)
+
+    def p1_own(p):
+        for r in (0, 1):
+            pl.when(xl == r)(lambda r=r: p1_send(p, r))
+
+    def p1_other(p):
+        for r in (0, 1):
+            pl.when(xl != r)(lambda r=r: p1_send(p, r))
 
     def p1_fwd(p, r):
         wait(p, r, 1, 0)
@@ -144,11 +159,11 @@
     barrier = pltpu.get_barrier_semaphore()
 
     def greet(i, carry):
-        other = lax.rem(s + i, N_SEQ)
+        other = xl * 16 + lax.rem(zy + i, 16)
         pl.semaphore_signal(barrier, inc=1, device_id=(other, h), device_id_type=MESH)
         return carry
 
-    lax.fori_loop(1, N_SEQ, greet, 0)
+    lax.fori_loop(1, 16, greet, 0)
     line = [(dx, dh) for dx in (0, 1) for dh in range(N_HEAD) if (dx, dh) != (0, 0)]
 
     def on_line(dx, dh):
@@ -157,17 +172,22 @@
         return ox, oh, (ox * 16 + zy, oh)
 
     for dx, dh in line:
-        if dh:
-            pl.semaphore_signal(barrier, inc=1, device_id=on_line(dx, dh)[2], device_id_type=MESH)
-    pl.semaphore_wait(barrier, N_SEQ - 1 + 6)
+        pl.semaphore_signal(barrier, inc=1, device_id=on_line(dx, dh)[2], device_id_type=MESH)
+    pl.semaphore_wait(barrier, 15 + 7)
 
     kv[xl, zy, 0:TOK, :] = k_ref[...]
     kv[xl, zy, TOK : 2 * TOK, :] = v_ref[...]
-    start(kv.at[xl, zy], kv.at[xl, zy], "xkv", (mate, h))
+
+    def same(ref):
+        return lambda: (ref, ref, (mate, h))
+
+    start(same(kv.at[xl, zy]), "xkv")
+    p1_own("kv")
+    dn_at = jnp.where(xl == 0, y * 4 + z, zy)
 
     low = lax.broadcasted_iota(jnp.int32, (FEAT, 128), 1) < 64
 
-    def pack(f, put_gu, put_dn):
+    def pack_gu(f, put):
         at = f * 768
         mid_gate = gate_ref[:, MAIN : MAIN + 128].astype(F32)
         mid_up = up_ref[:, MAIN : MAIN + 128].astype(F32)
@@ -175,31 +195,22 @@
             mixed = jnp.where(low, mid_gate, pltpu.roll(mid_up, 64, 1))
         else:
             mixed = jnp.where(low, pltpu.roll(mid_gate, 64, 1), mid_up)
-        put_gu(0, gate_ref[:, at : at + MAIN])
-        put_gu(MAIN, up_ref[:, at : at + MAIN])
-        put_gu(2 * MAIN, mixed.astype(BF16))
-        put_dn(down_ref[:, f * MAIN : f * MAIN + DNW])
+        put(0, gate_ref[:, at : at + MAIN])
+        put(MAIN, up_ref[:, at : at + MAIN])
+        put(2 * MAIN, mixed.astype(BF16))
 
     def own_gu(at, value):
         gu[xl, zy, :, at : at + value.shape[1]] = value
 
-    def own_dn(value):
-        dn[xl, zy] = value
-
     def mate_gu(at, value):
         sgu[:, at : at + value.shape[1]] = value
 
-    def mate_dn(value):
-        sdn[...] = value
-
     for f in (0, 1):
-
-        @pl.when(xl == f)
-        def _():
-            pack(1 - f, mate_gu, mate_dn)
-            pack(f, own_gu, own_dn)
-
-    start(sgu, gu.at[xl, zy], "xgu", (mate, h))
+        pl.when(xl == f)(lambda f=f: pack_gu(f, own_gu))
+    p1_own("gu")
+    for f in (0, 1):
+        pl.when(xl == f)(lambda f=f: pack_gu(1 - f, mate_gu))
+    start(lambda: (sgu, gu.at[xl, zy], (mate, h)), "xgu")
 
     share = jnp.cos((time_ref[...].astype(F32) / 1000.0 + 0.008) / 1.008 * (math.pi / 2.0)) ** 2
     signal, noise_part = jnp.sqrt(share), jnp.sqrt(1.0 - share)
@@ -209,13 +220,21 @@
     for n in range(NOISE):
         row = signal[:, n : n + 1] * clean_ref[...] + noise_part[:, n : n + 1] * noise_ref[:, n * LAT : (n + 1) * LAT]
         nz[xl, n * CAP : (n + 1) * CAP, 0:LAT] = row.astype(BF16)
-    start(nz.at[xl], nz.at[xl], "xnz", (mate, h))
-    start(tm.at[xl], tm.at[xl], "xtm", (mate, h))
+    start(same(nz.at[xl]), "xnz")
+    start(same(tm.at[xl]), "xtm")
 
     landed(kv.at[1 - xl, zy], "xkv", (mate, h))
-    both(p1_send, "kv")
+    p1_other("kv")
     both(p2_send, "kv", 0)
-    start(sdn, dn.at[xl, zy], "xdn", (mate, h))
+
+    for f in (0, 1):
+
+        @pl.when(xl == f)
+        def _():
+            sdn[...] = down_ref[:, (1 - f) * MAIN : (1 - f) * MAIN + DNW]
+            dn[xl, dn_at] = down_ref[:, f * MAIN : f * MAIN + DNW]
+
+    start(lambda: (sdn, dn.at[xl, dn_at], (mate, h)), "xdn")
 
     for j in range(GRP):
         cols = slice(j * HD, (j + 1) * HD)
@@ -228,7 +247,7 @@
     both(p2_send, "kv", 1)
     both(p2_send, "kv", 3)
     landed(gu.at[1 - xl, zy], "xgu", (mate, h))
-    both(p1_send, "gu")
+    p1_other("gu")
 
     steps = lax.broadcasted_iota(jnp.int32, (32, HALF), 0).astype(F32)
     for k, mult in ((0, 32.0), (2, 1.0)):
@@ -254,7 +273,8 @@
     lane = lax.broadcasted_iota(jnp.int32, (CAP, 128), 1)
     for b in (0, 1):
         for n in range(NOISE):
-            rows = slice((b * NOISE + n) * CAP, (b * NOISE + n + 1) * CAP)
+            place = (n % 2) * 4 + (n // 2) * 2 + b
+            rows = slice(place * CAP, (place + 1) * CAP)
             step = tm[b, :, n : n + 1]
             for ref, digit in ((oha, step >> 5), (ohb, step & 31)):
                 ref[rows, :] = jnp.where((lane & 31) == digit, jnp.where(lane < 96, 1.0, 0.0), 0.0).astype(BF16)
@@ -262,10 +282,14 @@
     both(p2_send, "gu", 1)
     both(p2_send, "gu", 3)
 
+    nz_rows = jnp.concatenate(
+        [nz[g % 2, ((g // 2 % 2) * 2 + g // 4) * CAP : ((g // 2 % 2) * 2 + g // 4 + 1) * CAP, 0:LAT] for g in range(8)], axis=0
+    )
+
     def embed(j, carry):
         c0 = pl.ds(pl.multiple_of(j * 256, 256), 256)
         c1 = pl.ds(pl.multiple_of(HALF + j * 256, 256), 256)
-        noisy = nz[...].reshape(2 * NOISE * CAP, 128)[:, 0:LAT]
+        noisy = nz_rows
         ca, sa = dot(oha[...], tab[0, :, c0]), dot(oha[...], tab[1, :, c0])
         cb, sb = dot(ohb[...], tab[2, :, c0]), dot(ohb[...], tab[3, :, c0])
         le[:, c0] = ca * cb - sa * sb + dot(noisy, lin_ref[:, c0])
@@ -278,7 +302,7 @@
         both(p2_fin, "kv", d)
     both(p1_fin, "gu")
     both(p2_send, "gu", 2)
-    landed(dn.at[1 - xl, zy], "xdn", (mate, h))
+    landed(dn.at[1 - xl, jnp.where(xl == 1, y * 4 + z, zy)], "xdn", (mate, h))
     both(p1_send, "dn")
 
     n_steps = lax.div(s, 2) + 1
@@ -348,12 +372,6 @@
 
     acc_t[...] = jnp.zeros_like(acc_t)
 
-    def term_copy(kb):
-        return pltpu.make_async_remote_copy(
-            src_ref=dkv.at[kb], dst_ref=drecv.at[s], send_sem=dssem.at[kb], recv_sem=drsem.at[s],
-            device_id=(kb, h), device_id_type=MESH,
-        )
-
     def grad_step(c, carry):
         keys, values = keys_of(c)
         prob = probs[pl.ds(pl.multiple_of(c * KC, KC), KC), :].astype(F32) * inverse
@@ -361,12 +379,6 @@
         acc_t[...] += contract_rows(keys, ds)
         dkv[pl.ds(2 * c, 2), 0:TOK, :] = (dot(ds, qs[...]) * SCALE).astype(BF16).reshape(2, TOK, HD)
         dkv[pl.ds(2 * c, 2), TOK : 2 * TOK, :] = dot(prob.astype(BF16), dos[...]).astype(BF16).reshape(2, TOK, HD)
-        for i in (0, 1):
-
-            @pl.when(2 * c + i < s)
-            def _():
-                term_copy(2 * c + i).start()
-
         return carry
 
     for part in range(4):
@@ -398,7 +410,7 @@
         square = jnp.zeros((CAP, 1), F32)
         for hh in range(N_HEAD):
             cols = slice(hh * HEADW, (hh + 1) * HEADW)
-            base = le[rows, cols] + cond[lax.div(g, NOISE), hh].astype(F32)
+            base = le[rows, cols] + cond[lax.rem(g, 2), hh].astype(F32)
             le[rows, cols] = base
             square += jnp.sum(base * base, axis=1, keepdims=True)
         scale = lax.rsqrt(square * (1.0 / D) + 1e-06)
@@ -440,68 +452,161 @@
         hid[:, 128:DNW] = (silu(acc[:, 0:MAIN]) * acc[:, MAIN : 2 * MAIN]).astype(BF16)
         hid[:, 0:128] = jnp.where(lower_half, 0.0, silu(turned) * mixed).astype(BF16)
 
-    for d in (0, 1, 3, 2):
-        both(p2_fin, "dn", d)
-
-    part_sent = []
+    def term_copy(b, kb):
+        return pltpu.make_async_remote_copy(
+            src_ref=dkv.at[b * 16 + kb], dst_ref=drecv.at[b, zy], send_sem=dssem.at[b * 16 + kb],
+            recv_sem=drsem.at[b * 16 + zy], device_id=(xl * 16 + kb, h), device_id_type=MESH,
+        )
+
+    def send_terms(kb, carry):
+        pl.when((kb != zy) & ((xl == 1) | (kb < zy)))(lambda: term_copy(0, kb).start())
+        pl.when((xl == 1) & (kb < zy))(lambda: term_copy(1, kb).start())
+        return carry
+
+    lax.fori_loop(0, 16, send_terms, 0)
+
+    def add_terms(b):
+        def step(i, run):
+            pltpu.make_async_remote_copy(
+                src_ref=drecv.at[b, i], dst_ref=drecv.at[b, i], send_sem=dssem.at[0], recv_sem=drsem.at[b * 16 + i],
+                device_id=(mate, h), device_id_type=MESH,
+            ).wait_recv()
+            return run + drecv[b, i].astype(F32)
+
+        return step
+
+    def along_x(step):
+        to = lax.rem(x + 4 + step, 4)
+        return (lax.rem(to, 2) * 16 + zy, lax.div(to, 2) * 2 + core)
+
+    def rows_of(place):
+        return pl.ds(pl.multiple_of(place * CAP, CAP), CAP)
+
+    def pick(step):
+        return lax.rem(x + 4 + step, 4) * CAP
+
+    SUB = 4 * FEAT
+    order = (0, 1, 3, 2)
+
+    def lanes(k):
+        return slice(k * 512, k * 512 + SUB)
+
+    def tot(k, r, step):
+        first = pl.multiple_of(r * 256 + pick(step), CAP)
+        return acc[pl.ds(first, CAP), lanes(k % 2)]
+
+    sibling = (s, h + 1 - 2 * core)
+
+    def stage0(k):
+        for r in (0, 1):
+            p2_fin("dn", r, order[k])
+        pieces = []
+        for r in (0, 1):
+            at = back(y if r == 0 else z, order[k]) * 4
+            piece = dn[r, pl.ds(at, 4)].reshape(SUB, DNW)
+            pieces.append(piece)
+            theirs = hid[pl.ds(pl.multiple_of((1 - core) * 256, 256), 256), :]
+            part = lax.dot_general(theirs, piece, (((1,), (1,)), ((), ())), preferred_element_type=F32)
+            s1[k, r] = part.astype(BF16)
+            start(lambda r=r: (s1.at[k, r], r1.at[k, r], sibling), ("r1", k, r))
+        for r in (0, 1):
+            ours = hid[pl.ds(pl.multiple_of(core * 256, 256), 256), :]
+            acc[r * 256 : r * 256 + 256, lanes(k % 2)] = lax.dot_general(ours, pieces[r], (((1,), (1,)), ((), ())), preferred_element_type=F32)
+
+    def stage1(k):
+        for r in (0, 1):
+            landed(r1.at[k, r], ("r1", k, r), sibling)
+            acc[r * 256 : r * 256 + 256, lanes(k % 2)] += r1[k, r].astype(F32)
+            s23[0, k, r] = tot(k, r, 2).astype(BF16)
+            start(lambda r=r: (s23.at[0, k, r], r2.at[k, r], along_x(1 - 2 * r)), ("r2", k, r))
+
+    def stage2(k):
+        for r in (0, 1):
+            landed(r2.at[k, r], ("r2", k, r), along_x(1))
+            for way, step in ((0, 1), (1, -1)):
+                near = tot(k, r, step)
+                if way == r:
+                    near += r2[k, r].astype(F32)
+                s23[1 + way, k, r] = near.astype(BF16)
+                start(
+                    lambda r=r, way=way, step=step: (s23.at[1 + way, k, r], r3.at[k, r, way], along_x(step)),
+                    ("r3", k, r, way),
+                )
+            fin[r, back(y if r == 0 else z, order[k])] = tot(k, r, 0)
+
+    def stage3(k):
+        for r in (0, 1):
+            at = back(y if r == 0 else z, order[k])
+            for way in (0, 1):
+                landed(r3.at[k, r, way], ("r3", k, r, way), along_x(1))
+                fin[r, at] += r3[k, r, way].astype(F32)
+
+    for k in range(6):
+        if 2 <= k:
+            stage2(k - 2)
+        if k < 4:
+            stage0(k)
+        if 1 <= k < 5:
+            stage1(k - 1)
+
+    @pl.when(xl == 1)
+    def _():
+        run = lax.fori_loop(0, zy, add_terms(0), dkv[zy].astype(F32))
+        run = lax.fori_loop(zy + 1, 16, add_terms(0), run)
+        xterm[0] = run.astype(BF16)
+
+    def cross():
+        return xterm.at[0], xterm.at[1], (mate, h)
+
+    pl.when(xl == 1)(lambda: copy_of(*cross()[:2], "xterm", cross()[2]).start())
+
     for k in range(4):
-        cols = slice(k * 896, (k + 1) * 896)
-        piece = dn[k // 2, (k % 2) * 8 : (k % 2) * 8 + 8].reshape(8 * FEAT, DNW)
-        part = lax.dot_general(hid[...], piece, (((1,), (1,)), ((), ())), preferred_element_type=F32)
-        nm[:, cols] = part.astype(BF16)
-        for i, (dx, dh) in enumerate(line):
-            ox, oh, dev = on_line(dx, dh)
-            rows = pl.ds(pl.multiple_of((ox * NOISE + oh) * CAP, CAP), CAP)
-            me = xl * N_HEAD + h
-            copy = pltpu.make_async_remote_copy(
-                src_ref=nm.at[rows, cols], dst_ref=rbuf.at[me, k], send_sem=fssem.at[k * 7 + i],
-                recv_sem=frsem.at[me * 4 + k], device_id=dev, device_id_type=MESH,
-            )
-            copy.start()
-            part_sent.append(copy)
-
-    def add_terms(i, run):
-        pltpu.make_async_remote_copy(
-            src_ref=drecv.at[i], dst_ref=drecv.at[i], send_sem=dssem.at[0], recv_sem=drsem.at[i],
-            device_id=(mate, h), device_id_type=MESH,
-        ).wait_recv()
-        return run + drecv[i].astype(F32)
-
-    terms = lax.fori_loop(s + 1, N_SEQ, add_terms, dkv[s].astype(F32))
-    dk_ref[...] = terms[0:TOK].astype(BF16)
-    dv_ref[...] = terms[TOK : 2 * TOK].astype(BF16)
-
-    own = pl.ds(pl.multiple_of((xl * NOISE + h) * CAP, CAP), CAP)
+        stage3(k)
+
+    def put_terms(run):
+        dk_ref[...] = run[0:TOK].astype(BF16)
+        dv_ref[...] = run[TOK : 2 * TOK].astype(BF16)
+
+    @pl.when(xl == 1)
+    def _():
+        put_terms(lax.fori_loop(zy + 1, 16, add_terms(1), dkv[16 + zy].astype(F32)))
+
+    own = rows_of(core * 4 + x)
+    for at in range(4):
+        for other in range(4):
+            c0 = other * SUB + at * FEAT
+            le[own, c0 : c0 + FEAT] += fin[0, at, :, other * FEAT : (other + 1) * FEAT]
+        c1 = HALF + at * SUB
+        le[own, c1 : c1 + SUB] += fin[1, at]
     square = jnp.zeros((CAP, 1), F32)
     for k in range(4):
-        cols = slice(k * 896, (k + 1) * 896)
-        rows = le[own, cols] + nm[own, cols].astype(F32)
-        for dx, dh in line:
-            ox, oh, dev = on_line(dx, dh)
-            src = ox * N_HEAD + oh
-            pltpu.make_async_remote_copy(
-                src_ref=rbuf.at[src, k], dst_ref=rbuf.at[src, k], send_sem=fssem.at[0],
-                recv_sem=frsem.at[src * 4 + k], device_id=dev, device_id_type=MESH,
-            ).wait_recv()
-            rows += rbuf[src, k].astype(F32)
-        le[own, cols] = rows
+        rows = le[own, k * 896 : (k + 1) * 896]
         square += jnp.sum(rows * rows, axis=1, keepdims=True)
     scale = lax.rsqrt(square * (1.0 / D) + 1e-06)
     result = jnp.zeros((CAP, LAT), F32)
     for k in range(4):
         cols = slice(k * 896, (k + 1) * 896)
         final = (le[own, cols] * scale * ogain_ref[:, cols]).astype(BF16)
-        result += dot(final, lout_ref[cols, :])
+        result += lax.dot_general(final, lout_ref[:, cols], (((1,), (1,)), ((), ())), preferred_element_type=F32)
     pred_ref[...] = jnp.where(valid, result, 0.0)
 
-    for copy in sent + cond_sent + part_sent:
+    @pl.when(xl == 0)
+    def _():
+        run = lax.fori_loop(zy + 1, 16, add_terms(0), dkv[zy].astype(F32))
+        landed(xterm.at[1], "xterm", (mate, h))
+        put_terms(run + xterm[1].astype(F32))
+
+    all_left()
+    pl.when(xl == 1)(lambda: copy_of(*cross()[:2], "xterm", cross()[2]).wait_send())
+    for copy in cond_sent:
         copy.wait_send()
 
-    def term_left(kb, carry):
-        term_copy(kb).wait_send()
+    def terms_left(kb, carry):
+        pl.when((kb != zy) & ((xl == 1) | (kb < zy)))(lambda: term_copy(0, kb).wait_send())
+        pl.when((xl == 1) & (kb < zy))(lambda: term_copy(1, kb).wait_send())
         return carry
 
-    lax.fori_loop(0, s, term_left, 0)
+    lax.fori_loop(0, 16, terms_left, 0)
 
 
 def shards(
@@ -511,7 +616,7 @@
     frequencies = np.exp(-math.log(10000.0) * np.arange(HALF, dtype=np.float32) / HALF).astype(np.float32)
     vmem = pl.BlockSpec(memory_space=pltpu.VMEM)
     dma = pltpu.SemaphoreType.DMA
-    n_sems = 140
+    n_sems = 176
     return pl.pallas_call(
         kernel,
         out_shape=(
@@ -536,7 +641,7 @@
             pltpu.VMEM((N_SEQ * TOK, ROWS), BF16),
             pltpu.VMEM((HD, ROWS), F32),
             pltpu.VMEM((N_SEQ, 2 * TOK, HD), BF16),
-            pltpu.VMEM((N_SEQ, 2 * TOK, HD), BF16),
+            pltpu.VMEM((2, 16, 2 * TOK, HD), BF16),
             pltpu.VMEM((2, N_HEAD, CAP, HEADW), BF16),
             pltpu.VMEM((2, NOISE * CAP, 128), BF16),
             pltpu.VMEM((2, CAP, 128), jnp.int32),
@@ -547,13 +652,17 @@
             pltpu.VMEM((2 * NOISE * CAP, D), BF16),
             pltpu.VMEM((2 * NOISE * CAP, GUW), F32),
             pltpu.VMEM((2 * NOISE * CAP, DNW), BF16),
-            pltpu.VMEM((8, 4, CAP, 896), BF16),
+            pltpu.VMEM((4, 2, 4 * CAP, 4 * FEAT), BF16),
+            pltpu.VMEM((3, 4, 2, CAP, 4 * FEAT), BF16),
+            pltpu.VMEM((4, 2, 4 * CAP, 4 * FEAT), BF16),
+            pltpu.VMEM((4, 2, CAP, 4 * FEAT), BF16),
+            pltpu.VMEM((4, 2, 2, CAP, 4 * FEAT), BF16),
+            pltpu.VMEM((2, 4, CAP, 4 * FEAT), F32),
+            pltpu.VMEM((2, 2 * TOK, HD), BF16),
             dma((n_sems,)),
             dma((n_sems,)),
             dma((N_SEQ,)),
             dma((N_SEQ,)),
-            dma((28,)),
-            dma((32,)),
             dma((7,)),
             dma((8,)),
         ],
@@ -563,7 +672,7 @@
     )(
         queries, key_vectors, value_vectors, out_cotangent, latent_mask.reshape(1, TOK), clean_latents, noise_draws,
         timesteps, latent_in, norm_gain.reshape(1, D), gate_weight, up_weight, down_weight, out_gain.reshape(1, D),
-        latent_out, jnp.asarray(frequencies.reshape(1, HALF)),
+        latent_out.T, jnp.asarray(frequencies.reshape(1, HALF)),
     )
 
 

time: 184 us -> 156 us (0.85)
  Pallas kernels: 170 us -> 146 us
  local copies, waits for them, and re-layouts: 9.61 us -> 7.33 us
    pallas_call x1, Pallas kernels: 170 us -> 146 us  [shards(): pl.pallas_call(kernel, out_shape=(jax.ShapeDtypeStruct((TOK, ROWS), BF16)...]
    unnamed x19 -> x18, local copies, waits for them, and re-layouts: 7.67 us -> 5.38 us
where the time goes in v2:
time: 156 us; the launch traced here: 154 us
  Pallas kernels  146 us (94%)
  local copies, waits for them, and re-layouts  7.33 us (5%)
    pallas_call x1, Pallas kernels, shards(): pl.pallas_call(kernel, out_shape=(jax.ShapeDtypeStruct((TOK, ROWS), BF16)...  146 us
    unnamed x18, local copies, waits for them, and re-layouts  5.38 us

profile of v2, /device:TPU:8, one launch (start us, length us, event | category | flops | bytes accessed | tf_op | source)
XLA Modules:
  0.0 154.0 jit_solution(8806185550692023125)
XLA Ops:
  0.6 0.0 copy-start.4
  0.6 1.3 reshape.20.ngain_ref
  2.0 0.0 copy-done.4
  2.0 0.0 copy-start.5
  2.0 0.6 reshape.21.ogain_ref
  2.6 0.1 copy-done.5
  2.7 0.7 copy.21.time_ref
  3.4 146.0 %shard_map.191 = (bf16[128,896]{1,0:T(8,128)(2,1)}, bf16[128,896]{1,0:T(8,128)(2,1)}, bf16[128,128]{1,0:T(8,128)(2,1)}, bf16[128,128]{1,0:T(8,128)(2,1)}, f32[64,64]{1,0:T(8,128)}) custom-call(bf16[128,896]{1,0:T(8,128)(2,1)} %q_ref.1, bf16[128,128]{1,0:T(8,128)(2,1)} %k_ref.1, bf16[128,128]{1,0:T(8,128)(2,1)} %v_ref.1, bf16[128,896]{1,0:T(8,128)(2,1)} %do_ref.1, ...), custom_call_target="tpu_custom_call" | custom-call | tf_op jit(solution)/shard_map/pallas_call | solution.py:620
  149.4 0.0 copy-start
  149.4 1.7 %copy.27 = bf16[128,896]{1,0:T(8,128)(2,1)} copy(bf16[128,896]{1,0:T(8,128)(2,1)} %get-tuple-element.10) | data formatting | bytes 458752
  151.1 0.0 copy-done
  151.1 0.0 copy-start.3
  151.1 0.7 copy.28
  151.8 0.1 copy-done.3
  151.9 0.0 copy-start.2
  151.9 0.6 copy.29
  152.5 0.2 copy-done.2
  152.7 0.0 copy-start.1
  152.7 0.6 copy.30
  153.3 0.2 copy-done.1
  153.4 0.6 copy.31
Async XLA Ops:
  0.6 1.3 copy-start.4
  2.0 0.7 copy-start.5
  149.4 1.7 %copy-start = (bf16[128,896]{1,0:T(8,128)(2,1)S(1)}, bf16[128,896]{1,0:T(8,128)(2,1)}, u32[]{:S(2)}) copy-start(bf16[128,896]{1,0:T(8,128)(2,1)} %get-tuple-element.11) | copy-start | bytes 688132
  151.1 0.8 copy-start.3
  151.9 0.8 copy-start.2
  152.7 0.8 copy-start.1

commit v3 on v2

--- a/solution.py
+++ b/solution.py
@@ -49,8 +49,8 @@
     gate_ref, up_ref, down_ref, ogain_ref, lout_ref, freq_ref,
     out_ref, dq_ref, dk_ref, dv_ref, pred_ref,
     kv, gu, dn, sgu, sdn, qs, qt, dos, dot_t, probs, acc_t, dkv, drecv, cond, nz, tm, tab, oha, ohb,
-    le, nm, acc, hid, s1, s23, r1, r2, r3, fin, xterm,
-    ssem, rsem, dssem, drsem, cssem, crsem,
+    le, nm, acc, hid, s1, s23, r1, r2, r3, fin, xterm, mterm,
+    ssem, rsem, dssem, drsem, cssem, crsem, xssem, xrsem,
 ):
     s = lax.axis_index("seq")
     h = lax.axis_index("head")
@@ -120,13 +120,17 @@
         send(p, r, 0, 0, 1, 1)
         send(p, r, 0, 0, 1, -1)
 
-    def p1_own(p):
+    def first_sends(p, r):
+        p1_send(p, r)
+        p2_send(p, r, 0)
+
+    def own(step, p, *rest):
         for r in (0, 1):
-            pl.when(xl == r)(lambda r=r: p1_send(p, r))
-
-    def p1_other(p):
+            pl.when(xl == r)(lambda r=r: step(p, r, *rest))
+
+    def other(step, p, *rest):
         for r in (0, 1):
-            pl.when(xl != r)(lambda r=r: p1_send(p, r))
+            pl.when(xl != r)(lambda r=r: step(p, r, *rest))
 
     def p1_fwd(p, r):
         wait(p, r, 1, 0)
@@ -158,12 +162,6 @@
 
     barrier = pltpu.get_barrier_semaphore()
 
-    def greet(i, carry):
-        other = xl * 16 + lax.rem(zy + i, 16)
-        pl.semaphore_signal(barrier, inc=1, device_id=(other, h), device_id_type=MESH)
-        return carry
-
-    lax.fori_loop(1, 16, greet, 0)
     line = [(dx, dh) for dx in (0, 1) for dh in range(N_HEAD) if (dx, dh) != (0, 0)]
 
     def on_line(dx, dh):
@@ -173,17 +171,10 @@
 
     for dx, dh in line:
         pl.semaphore_signal(barrier, inc=1, device_id=on_line(dx, dh)[2], device_id_type=MESH)
-    pl.semaphore_wait(barrier, 15 + 7)
-
-    kv[xl, zy, 0:TOK, :] = k_ref[...]
-    kv[xl, zy, TOK : 2 * TOK, :] = v_ref[...]
-
-    def same(ref):
-        return lambda: (ref, ref, (mate, h))
-
-    start(same(kv.at[xl, zy]), "xkv")
-    p1_own("kv")
-    dn_at = jnp.where(xl == 0, y * 4 + z, zy)
+    for axis in (1, 2):
+        for step in (1, -1):
+            pl.semaphore_signal(barrier, inc=1, device_id=neighbour(0, axis, step), device_id_type=MESH)
+    pl.semaphore_wait(barrier, 7 + 4)
 
     low = lax.broadcasted_iota(jnp.int32, (FEAT, 128), 1) < 64
 
@@ -205,36 +196,49 @@
     def mate_gu(at, value):
         sgu[:, at : at + value.shape[1]] = value
 
+    def same(ref):
+        return lambda: (ref, ref, (mate, h))
+
+    dn_at = jnp.where(xl == 0, y * 4 + z, zy)
+    kv[xl, zy, 0:TOK, :] = k_ref[...]
+    kv[xl, zy, TOK : 2 * TOK, :] = v_ref[...]
+    start(same(kv.at[xl, zy]), "xkv")
+    own(first_sends, "kv")
     for f in (0, 1):
         pl.when(xl == f)(lambda f=f: pack_gu(f, own_gu))
-    p1_own("gu")
+    own(first_sends, "gu")
     for f in (0, 1):
         pl.when(xl == f)(lambda f=f: pack_gu(1 - f, mate_gu))
     start(lambda: (sgu, gu.at[xl, zy], (mate, h)), "xgu")
-
-    share = jnp.cos((time_ref[...].astype(F32) / 1000.0 + 0.008) / 1.008 * (math.pi / 2.0)) ** 2
+    landed(kv.at[1 - xl, zy], "xkv", (mate, h))
+    other(first_sends, "kv")
+    own(p1_fwd, "kv")
+    own(p2_send, "kv", 1)
+    own(p2_send, "kv", 3)
+
+    for f in (0, 1):
+
+        @pl.when(xl == f)
+        def _():
+            sdn[...] = down_ref[:, (1 - f) * MAIN : (1 - f) * MAIN + DNW]
+            dn[xl, dn_at] = down_ref[:, f * MAIN : f * MAIN + DNW]
+
+    start(lambda: (sdn, dn.at[xl, dn_at], (mate, h)), "xdn")
+
+    digits = jnp.concatenate([time_ref[...] >> 5, time_ref[...] & 31], axis=0).astype(F32).astype(BF16)
+    unit = lax.broadcasted_iota(jnp.int32, (2 * NOISE, 128), 0) == lax.broadcasted_iota(jnp.int32, (2 * NOISE, 128), 1)
+    columns = contract_rows(digits, jnp.where(unit, 1.0, 0.0).astype(BF16))
+    steps_own = columns[:, 0:NOISE] * 32.0 + columns[:, NOISE : 2 * NOISE]
+    share = jnp.cos((steps_own / 1000.0 + 0.008) / 1.008 * (math.pi / 2.0)) ** 2
     signal, noise_part = jnp.sqrt(share), jnp.sqrt(1.0 - share)
     nz[xl] = jnp.zeros((NOISE * CAP, 128), BF16)
-    tm[xl] = jnp.zeros((CAP, 128), jnp.int32)
-    tm[xl, :, 0:NOISE] = time_ref[...]
+    tm[xl] = columns.astype(jnp.int32)
     for n in range(NOISE):
         row = signal[:, n : n + 1] * clean_ref[...] + noise_part[:, n : n + 1] * noise_ref[:, n * LAT : (n + 1) * LAT]
         nz[xl, n * CAP : (n + 1) * CAP, 0:LAT] = row.astype(BF16)
     start(same(nz.at[xl]), "xnz")
     start(same(tm.at[xl]), "xtm")
 
-    landed(kv.at[1 - xl, zy], "xkv", (mate, h))
-    p1_other("kv")
-    both(p2_send, "kv", 0)
-
-    for f in (0, 1):
-
-        @pl.when(xl == f)
-        def _():
-            sdn[...] = down_ref[:, (1 - f) * MAIN : (1 - f) * MAIN + DNW]
-            dn[xl, dn_at] = down_ref[:, f * MAIN : f * MAIN + DNW]
-
-    start(lambda: (sdn, dn.at[xl, dn_at], (mate, h)), "xdn")
 
     for j in range(GRP):
         cols = slice(j * HD, (j + 1) * HD)
@@ -243,11 +247,15 @@
         qt[:, cols] = q_ref[:, cols].astype(F32).T.astype(BF16)
         dot_t[:, cols] = do_ref[:, cols].astype(F32).T.astype(BF16)
 
-    both(p1_fwd, "kv")
-    both(p2_send, "kv", 1)
-    both(p2_send, "kv", 3)
     landed(gu.at[1 - xl, zy], "xgu", (mate, h))
-    p1_other("gu")
+    other(first_sends, "gu")
+    other(p1_fwd, "kv")
+    other(p2_send, "kv", 1)
+    other(p2_send, "kv", 3)
+    both(p1_fin, "kv")
+    both(p2_send, "kv", 2)
+    own(p1_fwd, "gu")
+    own(p2_send, "gu", 1)
 
     steps = lax.broadcasted_iota(jnp.int32, (32, HALF), 0).astype(F32)
     for k, mult in ((0, 32.0), (2, 1.0)):
@@ -261,12 +269,16 @@
             tab[kk, 64:96, :] = (rest - middle.astype(F32)).astype(BF16)
             tab[kk, 96:128, :] = jnp.zeros((32, HALF), BF16)
 
-    both(p1_fin, "kv")
-    both(p2_send, "kv", 2)
-    for d in (0, 1, 3, 2):
-        both(p2_fwd, "kv", d)
-    both(p1_fwd, "gu")
-    both(p2_send, "gu", 0)
+    both(p2_fwd, "kv", 0)
+    both(p2_fwd, "kv", 1)
+    own(p2_send, "gu", 3)
+    both(p2_fwd, "kv", 3)
+    both(p2_fwd, "kv", 2)
+    own(p1_fin, "gu")
+    other(p1_fwd, "gu")
+    other(p2_send, "gu", 1)
+    own(p2_send, "gu", 2)
+    other(p2_send, "gu", 3)
 
     landed(nz.at[1 - xl], "xnz", (mate, h))
     landed(tm.at[1 - xl], "xtm", (mate, h))
@@ -275,12 +287,8 @@
         for n in range(NOISE):
             place = (n % 2) * 4 + (n // 2) * 2 + b
             rows = slice(place * CAP, (place + 1) * CAP)
-            step = tm[b, :, n : n + 1]
-            for ref, digit in ((oha, step >> 5), (ohb, step & 31)):
+            for ref, digit in ((oha, tm[b, :, n : n + 1]), (ohb, tm[b, :, NOISE + n : NOISE + n + 1])):
                 ref[rows, :] = jnp.where((lane & 31) == digit, jnp.where(lane < 96, 1.0, 0.0), 0.0).astype(BF16)
-
-    both(p2_send, "gu", 1)
-    both(p2_send, "gu", 3)
 
     nz_rows = jnp.concatenate(
         [nz[g % 2, ((g // 2 % 2) * 2 + g // 4) * CAP : ((g // 2 % 2) * 2 + g // 4 + 1) * CAP, 0:LAT] for g in range(8)], axis=0
@@ -298,12 +306,13 @@
 
     lax.fori_loop(0, HALF // 256, embed, 0)
 
+    other(p1_fin, "gu")
+    other(p2_send, "gu", 2)
+    landed(dn.at[1 - xl, jnp.where(xl == 1, y * 4 + z, zy)], "xdn", (mate, h))
+    both(p1_send, "dn")
+    both(p2_fwd, "gu", 0)
     for d in (0, 1, 3, 2):
         both(p2_fin, "kv", d)
-    both(p1_fin, "gu")
-    both(p2_send, "gu", 2)
-    landed(dn.at[1 - xl, jnp.where(xl == 1, y * 4 + z, zy)], "xdn", (mate, h))
-    both(p1_send, "dn")
 
     n_steps = lax.div(s, 2) + 1
 
@@ -328,7 +337,8 @@
     row_max = lax.fori_loop(0, n_steps - 1, max_step, jnp.full((8, ROWS), NEG, F32))
     row_max = max_step(n_steps - 1, row_max, True)
     row_max = jnp.max(row_max, axis=0, keepdims=True)
-    both(p2_fwd, "gu", 0)
+    both(p2_fwd, "gu", 1)
+    both(p1_fwd, "dn")
 
     acc_t[...] = jnp.zeros_like(acc_t)
 
@@ -366,8 +376,7 @@
         copy.start()
         cond_sent.append(copy)
 
-    both(p2_fwd, "gu", 1)
-    both(p1_fwd, "dn")
+    both(p2_fwd, "gu", 3)
     both(p2_send, "dn", 0)
 
     acc_t[...] = jnp.zeros_like(acc_t)
@@ -381,16 +390,30 @@
         dkv[pl.ds(2 * c, 2), TOK : 2 * TOK, :] = dot(prob.astype(BF16), dos[...]).astype(BF16).reshape(2, TOK, HD)
         return carry
 
+    def crosses(kb):
+        return (kb < zy) | ((kb > zy) & (lax.rem(kb + zy, 2) == 1))
+
+    def cross_copy(kb):
+        return pltpu.make_async_remote_copy(
+            src_ref=dkv.at[kb], dst_ref=mterm.at[kb], send_sem=xssem.at[kb], recv_sem=xrsem.at[kb],
+            device_id=(mate, h), device_id_type=MESH,
+        )
+
     for part in range(4):
         lax.fori_loop(part * 4, jnp.minimum(n_steps, part * 4 + 4), grad_step, 0)
         if part == 0:
-            both(p2_fwd, "gu", 3)
+            both(p2_fwd, "gu", 2)
             both(p2_send, "dn", 1)
             both(p2_send, "dn", 3)
         elif part == 1:
-            both(p2_fwd, "gu", 2)
             both(p1_fin, "dn")
             both(p2_send, "dn", 2)
+
+            def send_cross(kb, carry):
+                pl.when((xl == 1) & crosses(kb))(lambda: cross_copy(kb).start())
+                return carry
+
+            lax.fori_loop(0, 16, send_cross, 0)
         elif part == 2:
             both(p2_fwd, "dn", 0)
 
@@ -416,11 +439,10 @@
         scale = lax.rsqrt(square * (1.0 / D) + 1e-06)
         for hh in range(N_HEAD):
             cols = slice(hh * HEADW, (hh + 1) * HEADW)
-            nm[rows, cols] = (le[rows, cols] * scale * ngain_ref[:, cols]).astype(BF16)
+            nm[rows, cols] = (le[rows, cols] * scale * ngain_ref[cols].reshape(1, HEADW)).astype(BF16)
         return carry
 
     lax.fori_loop(0, 2 * NOISE, norm_rows, 0)
-    both(p2_fwd, "dn", 1)
     for d in (0, 1, 3, 2):
         both(p2_fin, "gu", d)
 
@@ -432,12 +454,11 @@
         else:
             acc[...] += part
         if k == 1:
-            both(p2_fwd, "dn", 3)
+            both(p2_fwd, "dn", 1)
 
     def silu(value):
         return value / (1.0 + jnp.exp(-value))
 
-    both(p2_fwd, "dn", 2)
     mixed = acc[:, 2 * MAIN :]
     turned = pltpu.roll(mixed, 64, 1)
     lower_half = lax.broadcasted_iota(jnp.int32, (2 * NOISE * CAP, 128), 1) < 64
@@ -458,12 +479,40 @@
             recv_sem=drsem.at[b * 16 + zy], device_id=(xl * 16 + kb, h), device_id_type=MESH,
         )
 
+    def forward_copy(kb):
+        return pltpu.make_async_remote_copy(
+            src_ref=mterm.at[kb], dst_ref=drecv.at[0, zy], send_sem=dssem.at[kb], recv_sem=drsem.at[zy],
+            device_id=(kb, h), device_id_type=MESH,
+        )
+
+    def join_terms(kb, carry):
+        cross_copy(kb).wait_recv()
+        mterm[kb] = (mterm[kb].astype(F32) + dkv[kb].astype(F32)).astype(BF16)
+        forward_copy(kb).start()
+        return carry
+
+    def pass_terms(kb, carry):
+        @pl.when(lax.rem(kb + zy, 2) == 1)
+        def _():
+            cross_copy(kb).wait_recv()
+            forward_copy(kb).start()
+
+        return carry
+
     def send_terms(kb, carry):
-        pl.when((kb != zy) & ((xl == 1) | (kb < zy)))(lambda: term_copy(0, kb).start())
-        pl.when((xl == 1) & (kb < zy))(lambda: term_copy(1, kb).start())
+        pl.when((kb > zy) & (lax.rem(kb + zy, 2) == 0))(lambda: term_copy(0, kb).start())
+        pl.when(kb < zy)(lambda: term_copy(1, kb).start())
         return carry
 
-    lax.fori_loop(0, 16, send_terms, 0)
+    def all_terms():
+        @pl.when(xl == 0)
+        def _():
+            lax.fori_loop(0, zy, join_terms, 0)
+            lax.fori_loop(zy + 1, 16, pass_terms, 0)
+
+        @pl.when(xl == 1)
+        def _():
+            lax.fori_loop(0, 16, send_terms, 0)
 
     def add_terms(b):
         def step(i, run):
@@ -472,6 +521,12 @@
                 device_id=(mate, h), device_id_type=MESH,
             ).wait_recv()
             return run + drecv[b, i].astype(F32)
+
+        return step
+
+    def add_alternate(parity):
+        def step(i, run):
+            return lax.cond(lax.rem(i + zy, 2) == parity, lambda value: add_terms(0)(i, value), lambda value: value, run)
 
         return step
 
@@ -546,14 +601,16 @@
             stage2(k - 2)
         if k < 4:
             stage0(k)
+        if k < 2:
+            both(p2_fwd, "dn", order[k + 2])
+        if k == 1:
+            all_terms()
         if 1 <= k < 5:
             stage1(k - 1)
 
     @pl.when(xl == 1)
     def _():
-        run = lax.fori_loop(0, zy, add_terms(0), dkv[zy].astype(F32))
-        run = lax.fori_loop(zy + 1, 16, add_terms(0), run)
-        xterm[0] = run.astype(BF16)
+        xterm[0] = lax.fori_loop(0, zy, add_alternate(0), dkv[zy].astype(F32)).astype(BF16)
 
     def cross():
         return xterm.at[0], xterm.at[1], (mate, h)
@@ -586,13 +643,14 @@
     result = jnp.zeros((CAP, LAT), F32)
     for k in range(4):
         cols = slice(k * 896, (k + 1) * 896)
-        final = (le[own, cols] * scale * ogain_ref[:, cols]).astype(BF16)
+        final = (le[own, cols] * scale * ogain_ref[cols].reshape(1, 896)).astype(BF16)
         result += lax.dot_general(final, lout_ref[:, cols], (((1,), (1,)), ((), ())), preferred_element_type=F32)
     pred_ref[...] = jnp.where(valid, result, 0.0)
 
     @pl.when(xl == 0)
     def _():
         run = lax.fori_loop(zy + 1, 16, add_terms(0), dkv[zy].astype(F32))
+        run = lax.fori_loop(0, zy, add_alternate(1), run)
         landed(xterm.at[1], "xterm", (mate, h))
         put_terms(run + xterm[1].astype(F32))
 
@@ -602,11 +660,18 @@
         copy.wait_send()
 
     def terms_left(kb, carry):
-        pl.when((kb != zy) & ((xl == 1) | (kb < zy)))(lambda: term_copy(0, kb).wait_send())
+        pl.when((xl == 1) & crosses(kb))(lambda: cross_copy(kb).wait_send())
+        pl.when((xl == 0) & crosses(kb))(lambda: forward_copy(kb).wait_send())
+        pl.when((xl == 1) & (kb > zy) & (lax.rem(kb + zy, 2) == 0))(lambda: term_copy(0, kb).wait_send())
         pl.when((xl == 1) & (kb < zy))(lambda: term_copy(1, kb).wait_send())
         return carry
 
     lax.fori_loop(0, 16, terms_left, 0)
+
+
+def hand_over(*refs):
+    for i in range(5):
+        refs[5 + i][...] = refs[i][...]
 
 
 def shards(
@@ -617,7 +682,7 @@
     vmem = pl.BlockSpec(memory_space=pltpu.VMEM)
     dma = pltpu.SemaphoreType.DMA
     n_sems = 176
-    return pl.pallas_call(
+    results = pl.pallas_call(
         kernel,
         out_shape=(
             jax.ShapeDtypeStruct((TOK, ROWS), BF16),
@@ -659,21 +724,31 @@
             pltpu.VMEM((4, 2, 2, CAP, 4 * FEAT), BF16),
             pltpu.VMEM((2, 4, CAP, 4 * FEAT), F32),
             pltpu.VMEM((2, 2 * TOK, HD), BF16),
+            pltpu.VMEM((16, 2 * TOK, HD), BF16),
             dma((n_sems,)),
             dma((n_sems,)),
             dma((N_SEQ,)),
             dma((N_SEQ,)),
             dma((7,)),
             dma((8,)),
+            dma((16,)),
+            dma((16,)),
         ],
         compiler_params=pltpu.CompilerParams(
             collective_id=0, has_side_effects=True, vmem_limit_bytes=63 * 1024 * 1024
         ),
     )(
         queries, key_vectors, value_vectors, out_cotangent, latent_mask.reshape(1, TOK), clean_latents, noise_draws,
-        timesteps, latent_in, norm_gain.reshape(1, D), gate_weight, up_weight, down_weight, out_gain.reshape(1, D),
+        timesteps.T, latent_in, norm_gain, gate_weight, up_weight, down_weight, out_gain,
         latent_out.T, jnp.asarray(frequencies.reshape(1, HALF)),
     )
+    return pl.pallas_call(
+        hand_over,
+        out_shape=tuple(jax.ShapeDtypeStruct(a.shape, a.dtype) for a in results),
+        in_specs=[vmem] * 5,
+        out_specs=(vmem,) * 5,
+        compiler_params=pltpu.CompilerParams(vmem_limit_bytes=63 * 1024 * 1024),
+    )(*results)
 
 
 def solution(mesh):

time: 156 us -> 148 us (0.949); the launches traced: 154 us -> 148 us
  local copies, waits for them, and re-layouts: 7.33 us -> 0 us
  Pallas kernels: 146 us -> 148 us
    unnamed x18 -> x0, local copies, waits for them, and re-layouts: 5.38 us -> none
    reshape x2 -> x0, local copies, waits for them, and re-layouts: 1.94 us -> none  [the longest x1 1.33 us: shards(): norm_gain.reshape(1, D)]
    pallas_call x0 -> x1, Pallas kernels: none -> 1.88 us  [shards(): pl.pallas_call(hand_over, out_shape=tuple((jax.ShapeDtypeStruct(a.shape,...]
where the time goes in v3:
time: 148 us
  Pallas kernels  148 us (100%)
    pallas_call x1, Pallas kernels, shards(): pl.pallas_call(kernel, out_shape=(jax.ShapeDtypeStruct((TOK, ROWS), BF16)...  146 us

profile of v3, /device:TPU:8, one launch (start us, length us, event | category | flops | bytes accessed | tf_op | source)
XLA Modules:
  0.0 148.3 jit_solution(15981697984075126750)
XLA Ops:
  0.6 145.7 %shard_map.191 = (bf16[128,896]{1,0:T(8,128)(2,1)}, bf16[128,896]{1,0:T(8,128)(2,1)}, bf16[128,128]{1,0:T(8,128)(2,1)}, bf16[128,128]{1,0:T(8,128)(2,1)}, f32[64,64]{1,0:T(8,128)}) custom-call(bf16[128,896]{1,0:T(8,128)(2,1)} %q_ref.1, bf16[128,128]{1,0:T(8,128)(2,1)} %k_ref.1, bf16[128,128]{1,0:T(8,128)(2,1)} %v_ref.1, bf16[128,896]{1,0:T(8,128)(2,1)} %do_ref.1, ...), custom_call_target="tpu_custom_call" | custom-call | tf_op jit(solution)/shard_map/pallas_call | solution.py:685
  146.4 1.9 %shard_map.192 = (bf16[128,896]{1,0:T(8,128)(2,1)}, bf16[128,896]{1,0:T(8,128)(2,1)}, bf16[128,128]{1,0:T(8,128)(2,1)}, bf16[128,128]{1,0:T(8,128)(2,1)}, f32[64,64]{1,0:T(8,128)}) custom-call(bf16[128,896]{1,0:T(8,128)(2,1)} %get-tuple-element.10.refs_0_, bf16[128,896]{1,0:T(8,128)(2,1)} %get-tuple-element.11.refs_1_, ...), custom_call_target="tpu_custom_call" | custom-call | tf_op jit(solution)/shard_map/pallas_call | solution.py:745

commit v4 on v3

--- a/solution.py
+++ b/solution.py
@@ -49,7 +49,7 @@
     gate_ref, up_ref, down_ref, ogain_ref, lout_ref, freq_ref,
     out_ref, dq_ref, dk_ref, dv_ref, pred_ref,
     kv, gu, dn, sgu, sdn, qs, qt, dos, dot_t, probs, acc_t, dkv, drecv, cond, nz, tm, tab, oha, ohb,
-    le, nm, acc, hid, s1, s23, r1, r2, r3, fin, xterm, mterm,
+    le, nm, acc, hid, s1, s23, r1, r2, r3, fin, og, lo, mterm,
     ssem, rsem, dssem, drsem, cssem, crsem, xssem, xrsem,
 ):
     s = lax.axis_index("seq")
@@ -82,8 +82,16 @@
 
     def all_left():
         for key, make in leaving.items():
-            src, dst, dev = make()
-            copy_of(src, dst, key, dev).wait_send()
+            if key[:2] != ("kv", 1):
+                src, dst, dev = make()
+                copy_of(src, dst, key, dev).wait_send()
+
+        @pl.when(xl == 1)
+        def _():
+            for key, make in leaving.items():
+                if key[:2] == ("kv", 1):
+                    src, dst, dev = make()
+                    copy_of(src, dst, key, dev).wait_send()
 
     def back(pos, dist):
         return lax.rem(pos + 4 - dist, 4)
@@ -130,6 +138,8 @@
 
     def other(step, p, *rest):
         for r in (0, 1):
+            if p == "kv" and r == 1:
+                continue
             pl.when(xl != r)(lambda r=r: step(p, r, *rest))
 
     def p1_fwd(p, r):
@@ -158,7 +168,10 @@
 
     def both(step, p, *rest):
         step(p, 0, *rest)
-        step(p, 1, *rest)
+        if p == "kv":
+            pl.when(xl == 1)(lambda: step(p, 1, *rest))
+        else:
+            step(p, 1, *rest)
 
     barrier = pltpu.get_barrier_semaphore()
 
@@ -377,7 +390,6 @@
         cond_sent.append(copy)
 
     both(p2_fwd, "gu", 3)
-    both(p2_send, "dn", 0)
 
     acc_t[...] = jnp.zeros_like(acc_t)
 
@@ -390,9 +402,6 @@
         dkv[pl.ds(2 * c, 2), TOK : 2 * TOK, :] = dot(prob.astype(BF16), dos[...]).astype(BF16).reshape(2, TOK, HD)
         return carry
 
-    def crosses(kb):
-        return (kb < zy) | ((kb > zy) & (lax.rem(kb + zy, 2) == 1))
-
     def cross_copy(kb):
         return pltpu.make_async_remote_copy(
             src_ref=dkv.at[kb], dst_ref=mterm.at[kb], send_sem=xssem.at[kb], recv_sem=xrsem.at[kb],
@@ -403,23 +412,24 @@
         lax.fori_loop(part * 4, jnp.minimum(n_steps, part * 4 + 4), grad_step, 0)
         if part == 0:
             both(p2_fwd, "gu", 2)
+            both(p1_fin, "dn")
+            both(p2_send, "dn", 0)
             both(p2_send, "dn", 1)
-            both(p2_send, "dn", 3)
         elif part == 1:
-            both(p1_fin, "dn")
-            both(p2_send, "dn", 2)
 
             def send_cross(kb, carry):
-                pl.when((xl == 1) & crosses(kb))(lambda: cross_copy(kb).start())
+                cross_copy(kb).start()
                 return carry
 
-            lax.fori_loop(0, 16, send_cross, 0)
-        elif part == 2:
-            both(p2_fwd, "dn", 0)
+            @pl.when(xl == 1)
+            def _():
+                lax.fori_loop(0, 16, send_cross, 0)
 
     for j in range(GRP):
         cols = slice(j * HD, (j + 1) * HD)
         dq_ref[:, cols] = (acc_t[:, cols] * SCALE).T.astype(BF16)
+    both(p2_fwd, "dn", 0)
+    both(p2_send, "dn", 3)
 
     for dx, dh in line:
         ox, oh, dev = on_line(dx, dh)
@@ -443,8 +453,24 @@
         return carry
 
     lax.fori_loop(0, 2 * NOISE, norm_rows, 0)
+    both(p2_fwd, "dn", 1)
+    both(p2_send, "dn", 2)
     for d in (0, 1, 3, 2):
         both(p2_fin, "gu", d)
+
+    SUB = 4 * FEAT
+    mine = pl.ds(pl.multiple_of((core * 4 + x) * CAP, CAP), CAP)
+    for at in range(4):
+        for other_at in range(4):
+            c0 = other_at * SUB + at * FEAT
+            to = slice(other_at * FEAT, (other_at + 1) * FEAT)
+            fin[0, at, :, to] = le[mine, c0 : c0 + FEAT]
+            og[0, at, :, to] = jnp.broadcast_to(ogain_ref[c0 : c0 + FEAT].reshape(1, FEAT), (8, FEAT))
+            lo[0, at, :, to] = lout_ref[:, c0 : c0 + FEAT]
+        c1 = HALF + at * SUB
+        fin[1, at] = le[mine, c1 : c1 + SUB]
+        og[1, at] = jnp.broadcast_to(ogain_ref[c1 : c1 + SUB].reshape(1, SUB), (8, SUB))
+        lo[1, at] = lout_ref[:, c1 : c1 + SUB]
 
     for k in range(4):
         piece = gu[k // 2, (k % 2) * 8 : (k % 2) * 8 + 8].reshape(8 * FEAT, GUW)
@@ -453,8 +479,8 @@
             acc[...] = part
         else:
             acc[...] += part
-        if k == 1:
-            both(p2_fwd, "dn", 1)
+        if k == 2:
+            both(p2_fwd, "dn", 3)
 
     def silu(value):
         return value / (1.0 + jnp.exp(-value))
@@ -492,16 +518,12 @@
         return carry
 
     def pass_terms(kb, carry):
-        @pl.when(lax.rem(kb + zy, 2) == 1)
-        def _():
-            cross_copy(kb).wait_recv()
-            forward_copy(kb).start()
-
+        cross_copy(kb).wait_recv()
+        forward_copy(kb).start()
         return carry
 
     def send_terms(kb, carry):
-        pl.when((kb > zy) & (lax.rem(kb + zy, 2) == 0))(lambda: term_copy(0, kb).start())
-        pl.when(kb < zy)(lambda: term_copy(1, kb).start())
+        term_copy(1, kb).start()
         return carry
 
     def all_terms():
@@ -512,7 +534,7 @@
 
         @pl.when(xl == 1)
         def _():
-            lax.fori_loop(0, 16, send_terms, 0)
+            lax.fori_loop(0, zy, send_terms, 0)
 
     def add_terms(b):
         def step(i, run):
@@ -524,23 +546,13 @@
 
         return step
 
-    def add_alternate(parity):
-        def step(i, run):
-            return lax.cond(lax.rem(i + zy, 2) == parity, lambda value: add_terms(0)(i, value), lambda value: value, run)
-
-        return step
-
     def along_x(step):
         to = lax.rem(x + 4 + step, 4)
         return (lax.rem(to, 2) * 16 + zy, lax.div(to, 2) * 2 + core)
 
-    def rows_of(place):
-        return pl.ds(pl.multiple_of(place * CAP, CAP), CAP)
-
     def pick(step):
         return lax.rem(x + 4 + step, 4) * CAP
 
-    SUB = 4 * FEAT
     order = (0, 1, 3, 2)
 
     def lanes(k):
@@ -571,9 +583,11 @@
     def stage1(k):
         for r in (0, 1):
             landed(r1.at[k, r], ("r1", k, r), sibling)
+            far = r1[k, r, pl.ds(pl.multiple_of(pick(2), CAP), CAP), :].astype(F32)
+            s23[0, k, r] = (tot(k, r, 2) + far).astype(BF16)
+            start(lambda r=r: (s23.at[0, k, r], r2.at[k, r], along_x(1 - 2 * r)), ("r2", k, r))
+        for r in (0, 1):
             acc[r * 256 : r * 256 + 256, lanes(k % 2)] += r1[k, r].astype(F32)
-            s23[0, k, r] = tot(k, r, 2).astype(BF16)
-            start(lambda r=r: (s23.at[0, k, r], r2.at[k, r], along_x(1 - 2 * r)), ("r2", k, r))
 
     def stage2(k):
         for r in (0, 1):
@@ -587,7 +601,7 @@
                     lambda r=r, way=way, step=step: (s23.at[1 + way, k, r], r3.at[k, r, way], along_x(step)),
                     ("r3", k, r, way),
                 )
-            fin[r, back(y if r == 0 else z, order[k])] = tot(k, r, 0)
+            fin[r, back(y if r == 0 else z, order[k])] += tot(k, r, 0)
 
     def stage3(k):
         for r in (0, 1):
@@ -601,24 +615,27 @@
             stage2(k - 2)
         if k < 4:
             stage0(k)
-        if k < 2:
-            both(p2_fwd, "dn", order[k + 2])
-        if k == 1:
+        if k == 0:
+            both(p2_fwd, "dn", 2)
             all_terms()
         if 1 <= k < 5:
             stage1(k - 1)
 
-    @pl.when(xl == 1)
-    def _():
-        xterm[0] = lax.fori_loop(0, zy, add_alternate(0), dkv[zy].astype(F32)).astype(BF16)
-
-    def cross():
-        return xterm.at[0], xterm.at[1], (mate, h)
-
-    pl.when(xl == 1)(lambda: copy_of(*cross()[:2], "xterm", cross()[2]).start())
-
     for k in range(4):
         stage3(k)
+
+    square = jnp.zeros((CAP, 1), F32)
+    for r in (0, 1):
+        for at in range(4):
+            rows = fin[r, at]
+            square += jnp.sum(rows * rows, axis=1, keepdims=True)
+    scale = lax.rsqrt(square * (1.0 / D) + 1e-06)
+    result = jnp.zeros((CAP, LAT), F32)
+    for r in (0, 1):
+        for at in range(4):
+            final = (fin[r, at] * scale * og[r, at, 0:1, :]).astype(BF16)
+            result += lax.dot_general(final, lo[r, at], (((1,), (1,)), ((), ())), preferred_element_type=F32)
+    pred_ref[...] = jnp.where(valid, result, 0.0)
 
     def put_terms(run):
         dk_ref[...] = run[0:TOK].astype(BF16)
@@ -628,45 +645,33 @@
     def _():
         put_terms(lax.fori_loop(zy + 1, 16, add_terms(1), dkv[16 + zy].astype(F32)))
 
-    own = rows_of(core * 4 + x)
-    for at in range(4):
-        for other in range(4):
-            c0 = other * SUB + at * FEAT
-            le[own, c0 : c0 + FEAT] += fin[0, at, :, other * FEAT : (other + 1) * FEAT]
-        c1 = HALF + at * SUB
-        le[own, c1 : c1 + SUB] += fin[1, at]
-    square = jnp.zeros((CAP, 1), F32)
-    for k in range(4):
-        rows = le[own, k * 896 : (k + 1) * 896]
-        square += jnp.sum(rows * rows, axis=1, keepdims=True)
-    scale = lax.rsqrt(square * (1.0 / D) + 1e-06)
-    result = jnp.zeros((CAP, LAT), F32)
-    for k in range(4):
-        cols = slice(k * 896, (k + 1) * 896)
-        final = (le[own, cols] * scale * ogain_ref[cols].reshape(1, 896)).astype(BF16)
-        result += lax.dot_general(final, lout_ref[:, cols], (((1,), (1,)), ((), ())), preferred_element_type=F32)
-    pred_ref[...] = jnp.where(valid, result, 0.0)
-
     @pl.when(xl == 0)
     def _():
-        run = lax.fori_loop(zy + 1, 16, add_terms(0), dkv[zy].astype(F32))
-        run = lax.fori_loop(0, zy, add_alternate(1), run)
-        landed(xterm.at[1], "xterm", (mate, h))
-        put_terms(run + xterm[1].astype(F32))
+        cross_copy(zy).wait_recv()
+        run = dkv[zy].astype(F32) + mterm[zy].astype(F32)
+        run = lax.fori_loop(0, zy, add_terms(0), run)
+        put_terms(lax.fori_loop(zy + 1, 16, add_terms(0), run))
 
     all_left()
-    pl.when(xl == 1)(lambda: copy_of(*cross()[:2], "xterm", cross()[2]).wait_send())
     for copy in cond_sent:
         copy.wait_send()
 
-    def terms_left(kb, carry):
-        pl.when((xl == 1) & crosses(kb))(lambda: cross_copy(kb).wait_send())
-        pl.when((xl == 0) & crosses(kb))(lambda: forward_copy(kb).wait_send())
-        pl.when((xl == 1) & (kb > zy) & (lax.rem(kb + zy, 2) == 0))(lambda: term_copy(0, kb).wait_send())
-        pl.when((xl == 1) & (kb < zy))(lambda: term_copy(1, kb).wait_send())
-        return carry
-
-    lax.fori_loop(0, 16, terms_left, 0)
+    def left(copy):
+        def step(kb, carry):
+            copy(kb).wait_send()
+            return carry
+
+        return step
+
+    @pl.when(xl == 1)
+    def _():
+        lax.fori_loop(0, 16, left(cross_copy), 0)
+        lax.fori_loop(0, zy, left(lambda kb: term_copy(1, kb)), 0)
+
+    @pl.when(xl == 0)
+    def _():
+        lax.fori_loop(0, zy, left(forward_copy), 0)
+        lax.fori_loop(zy + 1, 16, left(forward_copy), 0)
 
 
 def hand_over(*refs):
@@ -723,7 +728,8 @@
             pltpu.VMEM((4, 2, CAP, 4 * FEAT), BF16),
             pltpu.VMEM((4, 2, 2, CAP, 4 * FEAT), BF16),
             pltpu.VMEM((2, 4, CAP, 4 * FEAT), F32),
-            pltpu.VMEM((2, 2 * TOK, HD), BF16),
+            pltpu.VMEM((2, 4, 8, 4 * FEAT), F32),
+            pltpu.VMEM((2, 4, LAT, 4 * FEAT), BF16),
             pltpu.VMEM((16, 2 * TOK, HD), BF16),
             dma((n_sems,)),
             dma((n_sems,)),

time: 148 us -> 149 us (level)
  no operation moved by 1% of the time
where the time goes in v4:
time: 149 us
  Pallas kernels  148 us (99%)
    pallas_call x1, Pallas kernels, shards(): pl.pallas_call(kernel, out_shape=(jax.ShapeDtypeStruct((TOK, ROWS), BF16)...  146 us

profile of v4, /device:TPU:8, one launch (start us, length us, event | category | flops | bytes accessed | tf_op | source)
XLA Modules:
  0.0 148.7 jit_solution(13312592136867576669)
XLA Ops:
  0.6 146.2 %shard_map.191 = (bf16[128,896]{1,0:T(8,128)(2,1)}, bf16[128,896]{1,0:T(8,128)(2,1)}, bf16[128,128]{1,0:T(8,128)(2,1)}, bf16[128,128]{1,0:T(8,128)(2,1)}, f32[64,64]{1,0:T(8,128)}) custom-call(bf16[128,896]{1,0:T(8,128)(2,1)} %q_ref.1, bf16[128,128]{1,0:T(8,128)(2,1)} %k_ref.1, bf16[128,128]{1,0:T(8,128)(2,1)} %v_ref.1, bf16[128,896]{1,0:T(8,128)(2,1)} %do_ref.1, ...), custom_call_target="tpu_custom_call" | custom-call | tf_op jit(solution)/shard_map/pallas_call | solution.py:690
  146.9 1.9 %shard_map.192 = (bf16[128,896]{1,0:T(8,128)(2,1)}, bf16[128,896]{1,0:T(8,128)(2,1)}, bf16[128,128]{1,0:T(8,128)(2,1)}, bf16[128,128]{1,0:T(8,128)(2,1)}, f32[64,64]{1,0:T(8,128)}) custom-call(bf16[128,896]{1,0:T(8,128)(2,1)} %get-tuple-element.10.refs_0_, bf16[128,896]{1,0:T(8,128)(2,1)} %get-tuple-element.11.refs_1_, ...), custom_call_target="tpu_custom_call" | custom-call | tf_op jit(solution)/shard_map/pallas_call | solution.py:751

commit v5 on v4

--- a/solution.py
+++ b/solution.py
@@ -45,13 +45,30 @@
 
 
 def kernel(
-    q_ref, k_ref, v_ref, do_ref, mask_ref, clean_ref, noise_ref, time_ref, lin_ref, ngain_ref,
-    gate_ref, up_ref, down_ref, ogain_ref, lout_ref, freq_ref,
+    q_hbm, k_ref, v_ref, do_hbm, mask_ref, clean_hbm, noise_hbm, time_ref, lin_hbm, ngain_ref,
+    gate_ref, up_ref, down_hbm, ogain_ref, lout_hbm, freq_ref,
     out_ref, dq_ref, dk_ref, dv_ref, pred_ref,
     kv, gu, dn, sgu, sdn, qs, qt, dos, dot_t, probs, acc_t, dkv, drecv, cond, nz, tm, tab, oha, ohb,
-    le, nm, acc, hid, s1, s23, r1, r2, r3, fin, og, lo, mterm,
-    ssem, rsem, dssem, drsem, cssem, crsem, xssem, xrsem,
+    le, nm, acc, hid, s1, s23, r1, r2, r3, fin, og, lo, mterm, tsum,
+    q_ref, do_ref, clean_ref, noise_ref, lin_ref, down_ref, lout_ref,
+    ssem, rsem, dssem, drsem, cssem, crsem, xssem, xrsem, fsem,
 ):
+    fetched = [
+        pltpu.make_async_copy(src, dst, fsem.at[i])
+        for i, (src, dst) in enumerate(
+            (
+                (down_hbm, down_ref),
+                (clean_hbm, clean_ref),
+                (noise_hbm, noise_ref),
+                (q_hbm, q_ref),
+                (do_hbm, do_ref),
+                (lin_hbm, lin_ref),
+                (lout_hbm, lout_ref),
+            )
+        )
+    ]
+    for copy in fetched:
+        copy.start()
     s = lax.axis_index("seq")
     h = lax.axis_index("head")
     xl = lax.div(s, 16)
@@ -229,6 +246,8 @@
     own(p2_send, "kv", 1)
     own(p2_send, "kv", 3)
 
+    for copy in fetched:
+        copy.wait()
     for f in (0, 1):
 
         @pl.when(xl == f)
@@ -428,8 +447,6 @@
     for j in range(GRP):
         cols = slice(j * HD, (j + 1) * HD)
         dq_ref[:, cols] = (acc_t[:, cols] * SCALE).T.astype(BF16)
-    both(p2_fwd, "dn", 0)
-    both(p2_send, "dn", 3)
 
     for dx, dh in line:
         ox, oh, dev = on_line(dx, dh)
@@ -453,8 +470,6 @@
         return carry
 
     lax.fori_loop(0, 2 * NOISE, norm_rows, 0)
-    both(p2_fwd, "dn", 1)
-    both(p2_send, "dn", 2)
     for d in (0, 1, 3, 2):
         both(p2_fin, "gu", d)
 
@@ -479,8 +494,12 @@
             acc[...] = part
         else:
             acc[...] += part
-        if k == 2:
-            both(p2_fwd, "dn", 3)
+        if k == 1:
+            both(p2_fwd, "dn", 0)
+            both(p2_send, "dn", 3)
+
+    both(p2_fwd, "dn", 1)
+    both(p2_send, "dn", 2)
 
     def silu(value):
         return value / (1.0 + jnp.exp(-value))
@@ -511,40 +530,40 @@
             device_id=(kb, h), device_id_type=MESH,
         )
 
-    def join_terms(kb, carry):
-        cross_copy(kb).wait_recv()
-        mterm[kb] = (mterm[kb].astype(F32) + dkv[kb].astype(F32)).astype(BF16)
-        forward_copy(kb).start()
-        return carry
-
-    def pass_terms(kb, carry):
-        cross_copy(kb).wait_recv()
-        forward_copy(kb).start()
-        return carry
-
-    def send_terms(kb, carry):
-        term_copy(1, kb).start()
-        return carry
-
-    def all_terms():
-        @pl.when(xl == 0)
-        def _():
-            lax.fori_loop(0, zy, join_terms, 0)
-            lax.fori_loop(zy + 1, 16, pass_terms, 0)
-
-        @pl.when(xl == 1)
-        def _():
-            lax.fori_loop(0, zy, send_terms, 0)
-
-    def add_terms(b):
-        def step(i, run):
-            pltpu.make_async_remote_copy(
-                src_ref=drecv.at[b, i], dst_ref=drecv.at[b, i], send_sem=dssem.at[0], recv_sem=drsem.at[b * 16 + i],
-                device_id=(mate, h), device_id_type=MESH,
-            ).wait_recv()
-            return run + drecv[b, i].astype(F32)
-
-        return step
+    def some_terms(first, last):
+        def step(i, carry):
+            kb = lax.rem(zy + i, 16)
+
+            @pl.when(xl == 0)
+            def _():
+                cross_copy(kb).wait_recv()
+
+                @pl.when(kb < zy)
+                def _():
+                    mterm[kb] = (mterm[kb].astype(F32) + dkv[kb].astype(F32)).astype(BF16)
+
+                forward_copy(kb).start()
+
+            pl.when((xl == 1) & (kb < zy))(lambda: term_copy(1, kb).start())
+            return carry
+
+        lax.fori_loop(first, last, step, 0)
+
+    def add_terms(first, last):
+        def step(i, carry):
+            src = lax.rem(zy + 16 - i, 16)
+
+            @pl.when((xl == 0) | (src > zy))
+            def _():
+                pltpu.make_async_remote_copy(
+                    src_ref=drecv.at[xl, src], dst_ref=drecv.at[xl, src], send_sem=dssem.at[0],
+                    recv_sem=drsem.at[xl * 16 + src], device_id=(mate, h), device_id_type=MESH,
+                ).wait_recv()
+                tsum[...] += drecv[xl, src].astype(F32)
+
+            return carry
+
+        lax.fori_loop(first, last, step, 0)
 
     def along_x(step):
         to = lax.rem(x + 4 + step, 4)
@@ -610,17 +629,24 @@
                 landed(r3.at[k, r, way], ("r3", k, r, way), along_x(1))
                 fin[r, at] += r3[k, r, way].astype(F32)
 
-    for k in range(6):
-        if 2 <= k:
-            stage2(k - 2)
-        if k < 4:
-            stage0(k)
-        if k == 0:
-            both(p2_fwd, "dn", 2)
-            all_terms()
-        if 1 <= k < 5:
-            stage1(k - 1)
-
+    stage0(0)
+    both(p2_fwd, "dn", 3)
+    stage1(0)
+    stage0(1)
+    stage2(0)
+    stage1(1)
+    both(p2_fwd, "dn", 2)
+    some_terms(1, 16)
+    stage2(1)
+    stage0(2)
+    stage1(2)
+    stage0(3)
+    stage2(2)
+    stage1(3)
+    tsum[...] = dkv[s].astype(F32)
+    add_terms(1, 4)
+    stage2(3)
+    add_terms(4, 8)
     for k in range(4):
         stage3(k)
 
@@ -637,20 +663,14 @@
             result += lax.dot_general(final, lo[r, at], (((1,), (1,)), ((), ())), preferred_element_type=F32)
     pred_ref[...] = jnp.where(valid, result, 0.0)
 
-    def put_terms(run):
-        dk_ref[...] = run[0:TOK].astype(BF16)
-        dv_ref[...] = run[TOK : 2 * TOK].astype(BF16)
-
-    @pl.when(xl == 1)
-    def _():
-        put_terms(lax.fori_loop(zy + 1, 16, add_terms(1), dkv[16 + zy].astype(F32)))
-
     @pl.when(xl == 0)
     def _():
         cross_copy(zy).wait_recv()
-        run = dkv[zy].astype(F32) + mterm[zy].astype(F32)
-        run = lax.fori_loop(0, zy, add_terms(0), run)
-        put_terms(lax.fori_loop(zy + 1, 16, add_terms(0), run))
+        tsum[...] += mterm[zy].astype(F32)
+
+    add_terms(8, 16)
+    dk_ref[...] = tsum[0:TOK].astype(BF16)
+    dv_ref[...] = tsum[TOK : 2 * TOK].astype(BF16)
 
     all_left()
     for copy in cond_sent:
@@ -685,6 +705,7 @@
 ):
     frequencies = np.exp(-math.log(10000.0) * np.arange(HALF, dtype=np.float32) / HALF).astype(np.float32)
     vmem = pl.BlockSpec(memory_space=pltpu.VMEM)
+    hbm = pl.BlockSpec(memory_space=pl.ANY)
     dma = pltpu.SemaphoreType.DMA
     n_sems = 176
     results = pl.pallas_call(
@@ -696,7 +717,7 @@
             jax.ShapeDtypeStruct((TOK, HD), BF16),
             jax.ShapeDtypeStruct((CAP, LAT), F32),
         ),
-        in_specs=[vmem] * 16,
+        in_specs=[hbm if i in (0, 3, 5, 6, 8, 12, 14) else vmem for i in range(16)],
         out_specs=(vmem,) * 5,
         scratch_shapes=[
             pltpu.VMEM((2, 16, 2 * TOK, HD), BF16),
@@ -731,6 +752,14 @@
             pltpu.VMEM((2, 4, 8, 4 * FEAT), F32),
             pltpu.VMEM((2, 4, LAT, 4 * FEAT), BF16),
             pltpu.VMEM((16, 2 * TOK, HD), BF16),
+            pltpu.VMEM((2 * TOK, HD), F32),
+            pltpu.VMEM((TOK, ROWS), BF16),
+            pltpu.VMEM((TOK, ROWS), BF16),
+            pltpu.VMEM((CAP, LAT), F32),
+            pltpu.VMEM((CAP, NOISE * LAT), F32),
+            pltpu.VMEM((LAT, D), BF16),
+            pltpu.VMEM((FEAT, 1408), BF16),
+            pltpu.VMEM((LAT, D), BF16),
             dma((n_sems,)),
             dma((n_sems,)),
             dma((N_SEQ,)),
@@ -739,6 +768,7 @@
             dma((8,)),
             dma((16,)),
             dma((16,)),
+            dma((7,)),
         ],
         compiler_params=pltpu.CompilerParams(
             collective_id=0, has_side_effects=True, vmem_limit_bytes=63 * 1024 * 1024

time: 149 us -> 139 us (0.933)
  the two profiles are of different devices: /device:TPU:8 before, /device:TPU:2 now
where the time goes in v5:
time: 139 us
  Pallas kernels  138 us (99%)
    pallas_call x1, Pallas kernels, shards(): pl.pallas_call(kernel, out_shape=(jax.ShapeDtypeStruct((TOK, ROWS), BF16)...  137 us

profile of v5, /device:TPU:2, one launch (start us, length us, event | category | flops | bytes accessed | tf_op | source)
XLA Modules:
  0.0 139.1 jit_solution(16999968495284675746)
XLA Ops:
  0.6 136.6 %shard_map.191 = (bf16[128,896]{1,0:T(8,128)(2,1)}, bf16[128,896]{1,0:T(8,128)(2,1)}, bf16[128,128]{1,0:T(8,128)(2,1)}, bf16[128,128]{1,0:T(8,128)(2,1)}, f32[64,64]{1,0:T(8,128)}) custom-call(bf16[128,896]{1,0:T(8,128)(2,1)} %q_hbm.1, bf16[128,128]{1,0:T(8,128)(2,1)} %k_ref.1, bf16[128,128]{1,0:T(8,128)(2,1)} %v_ref.1, bf16[128,896]{1,0:T(8,128)(2,1)} %do_hbm.1, ...), custom_call_target="tpu_custom_call" | custom-call | tf_op jit(solution)/shard_map/pallas_call | solution.py:711
  137.3 1.9 %shard_map.192 = (bf16[128,896]{1,0:T(8,128)(2,1)}, bf16[128,896]{1,0:T(8,128)(2,1)}, bf16[128,128]{1,0:T(8,128)(2,1)}, bf16[128,128]{1,0:T(8,128)(2,1)}, f32[64,64]{1,0:T(8,128)}) custom-call(bf16[128,896]{1,0:T(8,128)(2,1)} %get-tuple-element.10.refs_0_, bf16[128,896]{1,0:T(8,128)(2,1)} %get-tuple-element.11.refs_1_, ...), custom_call_target="tpu_custom_call" | custom-call | tf_op jit(solution)/shard_map/pallas_call | solution.py:781

commit v6 on v5

--- a/solution.py
+++ b/solution.py
@@ -49,9 +49,9 @@
     gate_ref, up_ref, down_hbm, ogain_ref, lout_hbm, freq_ref,
     out_ref, dq_ref, dk_ref, dv_ref, pred_ref,
     kv, gu, dn, sgu, sdn, qs, qt, dos, dot_t, probs, acc_t, dkv, drecv, cond, nz, tm, tab, oha, ohb,
-    le, nm, acc, hid, s1, s23, r1, r2, r3, fin, og, lo, mterm, tsum,
+    le, nm, acc, hid, s1, s23, r1, r2, r3, fin, og, lo, mterm, tsum, rterm,
     q_ref, do_ref, clean_ref, noise_ref, lin_ref, down_ref, lout_ref,
-    ssem, rsem, dssem, drsem, cssem, crsem, xssem, xrsem, fsem,
+    ssem, rsem, dssem, drsem, cssem, crsem, xssem, xrsem, fsem, rssem, rrsem,
 ):
     fetched = [
         pltpu.make_async_copy(src, dst, fsem.at[i])
@@ -434,7 +434,9 @@
             both(p1_fin, "dn")
             both(p2_send, "dn", 0)
             both(p2_send, "dn", 1)
-        elif part == 1:
+        if part == 2:
+            both(p2_send, "dn", 3)
+        if part < 2:
 
             def send_cross(kb, carry):
                 cross_copy(kb).start()
@@ -442,7 +444,7 @@
 
             @pl.when(xl == 1)
             def _():
-                lax.fori_loop(0, 16, send_cross, 0)
+                lax.fori_loop(part * 8, part * 8 + 8, send_cross, 0)
 
     for j in range(GRP):
         cols = slice(j * HD, (j + 1) * HD)
@@ -496,7 +498,6 @@
             acc[...] += part
         if k == 1:
             both(p2_fwd, "dn", 0)
-            both(p2_send, "dn", 3)
 
     both(p2_fwd, "dn", 1)
     both(p2_send, "dn", 2)
@@ -534,26 +535,71 @@
         def step(i, carry):
             kb = lax.rem(zy + i, 16)
 
-            @pl.when(xl == 0)
-            def _():
-                cross_copy(kb).wait_recv()
-
-                @pl.when(kb < zy)
-                def _():
-                    mterm[kb] = (mterm[kb].astype(F32) + dkv[kb].astype(F32)).astype(BF16)
-
-                forward_copy(kb).start()
-
             pl.when((xl == 1) & (kb < zy))(lambda: term_copy(1, kb).start())
             return carry
 
         lax.fori_loop(first, last, step, 0)
+
+    def term_at(dz, dy):
+        return lax.rem(z + dz, 4) * 4 + lax.rem(y + dy, 4)
+
+    def relay_copy(dz):
+        return pltpu.make_async_remote_copy(
+            src_ref=mterm.at[term_at(dz, 2)], dst_ref=rterm.at[dz], send_sem=rssem.at[dz], recv_sem=rrsem.at[dz],
+            device_id=(z * 4 + back(y, 1), h), device_id_type=MESH,
+        )
+
+    def ready_term(dz, dy):
+        kb = term_at(dz, dy)
+        cross_copy(kb).wait_recv()
+
+        @pl.when(kb < zy)
+        def _():
+            mterm[kb] = (mterm[kb].astype(F32) + dkv[kb].astype(F32)).astype(BF16)
+
+        return kb
+
+    def plane_terms():
+        def far(dz, carry):
+            ready_term(dz, 2)
+            relay_copy(dz).start()
+            return carry
+
+        def near(dz, carry):
+            forward_copy(ready_term(dz, 1)).start()
+            return carry
+
+        def column(dz, carry):
+            forward_copy(ready_term(dz, 0)).start()
+            return carry
+
+        def joined(dz, carry):
+            kb = ready_term(dz, 3)
+            relay_copy(dz).wait_recv()
+            mterm[kb] = (mterm[kb].astype(F32) + rterm[dz].astype(F32)).astype(BF16)
+            forward_copy(kb).start()
+            return carry
+
+        lax.fori_loop(0, 4, far, 0)
+        lax.fori_loop(0, 4, near, 0)
+        lax.fori_loop(1, 4, column, 0)
+        lax.fori_loop(0, 4, joined, 0)
+
+    def plane_terms_left():
+        def step(dz, carry):
+            relay_copy(dz).wait_send()
+            forward_copy(term_at(dz, 1)).wait_send()
+            pl.when(dz > 0)(lambda: forward_copy(term_at(dz, 0)).wait_send())
+            forward_copy(term_at(dz, 3)).wait_send()
+            return carry
+
+        lax.fori_loop(0, 4, step, 0)
 
     def add_terms(first, last):
         def step(i, carry):
             src = lax.rem(zy + 16 - i, 16)
 
-            @pl.when((xl == 0) | (src > zy))
+            @pl.when(((xl == 0) & (lax.rem(y + 4 - lax.rem(src, 4), 4) != 2)) | ((xl == 1) & (src > zy)))
             def _():
                 pltpu.make_async_remote_copy(
                     src_ref=drecv.at[xl, src], dst_ref=drecv.at[xl, src], send_sem=dssem.at[0],
@@ -637,6 +683,7 @@
     stage1(1)
     both(p2_fwd, "dn", 2)
     some_terms(1, 16)
+    pl.when(xl == 0)(plane_terms)
     stage2(1)
     stage0(2)
     stage1(2)
@@ -690,8 +737,7 @@
 
     @pl.when(xl == 0)
     def _():
-        lax.fori_loop(0, zy, left(forward_copy), 0)
-        lax.fori_loop(zy + 1, 16, left(forward_copy), 0)
+        plane_terms_left()
 
 
 def hand_over(*refs):
@@ -753,6 +799,7 @@
             pltpu.VMEM((2, 4, LAT, 4 * FEAT), BF16),
             pltpu.VMEM((16, 2 * TOK, HD), BF16),
             pltpu.VMEM((2 * TOK, HD), F32),
+            pltpu.VMEM((4, 2 * TOK, HD), BF16),
             pltpu.VMEM((TOK, ROWS), BF16),
             pltpu.VMEM((TOK, ROWS), BF16),
             pltpu.VMEM((CAP, LAT), F32),
@@ -769,6 +816,8 @@
             dma((16,)),
             dma((16,)),
             dma((7,)),
+            dma((4,)),
+            dma((4,)),
         ],
         compiler_params=pltpu.CompilerParams(
             collective_id=0, has_side_effects=True, vmem_limit_bytes=63 * 1024 * 1024

time: 139 us -> 139 us (level)
  the two profiles are of different devices: /device:TPU:2 before, /device:TPU:8 now
where the time goes in v6:
time: 139 us; the launch traced here: 136 us
  Pallas kernels  136 us (98%)
    pallas_call x1, Pallas kernels, shards(): pl.pallas_call(kernel, out_shape=(jax.ShapeDtypeStruct((TOK, ROWS), BF16)...  134 us

profile of v6, /device:TPU:8, one launch (start us, length us, event | category | flops | bytes accessed | tf_op | source)
XLA Modules:
  0.0 136.3 jit_solution(11419167004514834089)
XLA Ops:
  0.6 133.8 %shard_map.191 = (bf16[128,896]{1,0:T(8,128)(2,1)}, bf16[128,896]{1,0:T(8,128)(2,1)}, bf16[128,128]{1,0:T(8,128)(2,1)}, bf16[128,128]{1,0:T(8,128)(2,1)}, f32[64,64]{1,0:T(8,128)}) custom-call(bf16[128,896]{1,0:T(8,128)(2,1)} %q_hbm.1, bf16[128,128]{1,0:T(8,128)(2,1)} %k_ref.1, bf16[128,128]{1,0:T(8,128)(2,1)} %v_ref.1, bf16[128,896]{1,0:T(8,128)(2,1)} %do_hbm.1, ...), custom_call_target="tpu_custom_call" | custom-call | tf_op jit(solution)/shard_map/pallas_call | solution.py:757
  134.4 1.9 %shard_map.192 = (bf16[128,896]{1,0:T(8,128)(2,1)}, bf16[128,896]{1,0:T(8,128)(2,1)}, bf16[128,128]{1,0:T(8,128)(2,1)}, bf16[128,128]{1,0:T(8,128)(2,1)}, f32[64,64]{1,0:T(8,128)}) custom-call(bf16[128,896]{1,0:T(8,128)(2,1)} %get-tuple-element.10.refs_0_, bf16[128,896]{1,0:T(8,128)(2,1)} %get-tuple-element.11.refs_1_, ...), custom_call_target="tpu_custom_call" | custom-call | tf_op jit(solution)/shard_map/pallas_call | solution.py:830
